TPU v7x, 512 devices: a whole 4x8x8 slice. The times are simulated.
512 devices in a mesh: group: 32 (over x_lo, z, core), tensor: 16 (over y, x_hi).
Axes of the slice: x: 4 (x_hi: 2, x_lo: 2; x = x_hi * 2 + x_lo), y: 8, z: 8, core: 2. Of those that a mesh axis runs over, the one named last changes fastest.
Arguments:
- hidden_x: bfloat16 [64, 8, 8192], P('group', None, 'tensor'), may hold values from -6 to 6
- base_weight: bfloat16 [2048, 8192], P(None, 'tensor'), may hold values from -0.0625 to 0.0625
- delta_codes: bfloat16 [2048, 8192], P('group', 'tensor'), may hold values from -4 to 4
- delta_scales: bfloat16 [2048, 64], P('group', 'tensor'), may hold values from 0.0019989014 to 0.019897461
- owner_map: int32 [32], replicated, may hold values from 0 to 31, each once
- kv_cache: bfloat16 [64, 4096, 2048], P('group', 'tensor'), may hold values from -6 to 6
- queries: bfloat16 [64, 8, 8192], P('group'), may hold values from -180 to 180
- lengths: int32 [64], P('group'), may hold values from 1024 to 4096, as said below
Outputs:
- new_kv: bfloat16 [64, 8, 2048], P('group', None, 'tensor')
- attended: bfloat16 [64, 8, 8192], P('group', None, 'tensor')
Inputs may be any that keep to these rules, and one draw needn't show every extreme that they name: `owner_map`: a permutation of the shard indices. Row r's entries are its first lengths[r] cache positions; some row is full.
All inputs are finite; a program needn't handle non-finite values.
Results may differ from a plain program's by a relative error of at most 0.009.
Values may be sent and summed in bfloat16 or wider, within the bound.
A program may use at most 64 MiB of HBM per device.

v0:
```python
import jax
import jax.numpy as jnp
from jax import lax
from jax.sharding import PartitionSpec as P

H = 64
KVH = 8
HD = 128


NEGATIVE = -1e30


def joined_2(x, axis, combine):
    everything = jax.tree.map(lambda part: lax.all_gather(part, axis), x)
    initial = jax.tree.map(lambda part: part[0], everything)

    def step(k, so_far):
        return combine(so_far, jax.tree.map(lambda part: part[k], everything))

    return lax.fori_loop(1, lax.axis_size(axis), step, initial)


def dequantize(code_values, block_scales):
    blocks = block_scales.shape[1]
    widened = code_values.astype(jnp.float32).reshape(code_values.shape[0], blocks, -1)
    return (
        (widened * block_scales.astype(jnp.float32)[:, :, None])
        .reshape(code_values.shape[0], -1)
        .astype(jnp.bfloat16)
    )


def combine(left_part, right_part):
    left_peak, left_total, left_sum = left_part
    right_peak, right_total, right_sum = right_part
    joined = jnp.maximum(left_peak, right_peak)
    left_scale = jnp.exp(left_peak - joined)
    right_scale = jnp.exp(right_peak - joined)
    return (
        joined,
        left_total * left_scale + right_total * right_scale,
        left_sum * left_scale[..., None] + right_sum * right_scale[..., None],
    )


def on_device(
    hidden_x, base_weight, delta_codes, delta_scales, owner_map, kv_cache, queries, lengths
):
    score_scale = HD ** (-0.5)
    kv_width = KVH * HD
    per_group = H // KVH
    group_count = lax.axis_size("group")
    tensor_count = lax.axis_size("tensor")
    tensor_place = lax.axis_index("tensor")
    row_count, step_count, local_width = hidden_x.shape
    token_rows = hidden_x.reshape(row_count * step_count, local_width)
    base_part = jnp.einsum("rd,od->ro", token_rows, base_weight, preferred_element_type=jnp.float32)
    codes_all, scales_all = (
        lax.all_gather(delta_codes, "group", axis=0, tiled=True),
        lax.all_gather(delta_scales, "group", axis=0, tiled=True),
    )
    delta_part = jnp.einsum(
        "rd,od->ro",
        token_rows,
        dequantize(codes_all, scales_all),
        preferred_element_type=jnp.float32,
    )
    owner_block = delta_part.shape[1] // group_count
    reorder = (owner_map[:, None] == jnp.arange(group_count, dtype=jnp.int32)[None, :]).astype(
        jnp.float32
    )
    ordered = jnp.einsum(
        "rgo,gb->rbo",
        delta_part.reshape(-1, group_count, owner_block),
        reorder,
        precision=lax.Precision.HIGHEST,
    ).reshape(delta_part.shape)
    summed = lax.psum(base_part + ordered, "tensor")
    new_all = summed.astype(jnp.bfloat16).reshape(row_count, step_count, -1)
    slice_width = new_all.shape[2] // tensor_count
    new_out = lax.dynamic_slice_in_dim(new_all, tensor_place * slice_width, slice_width, 2)
    grouped_query = queries.reshape(row_count, step_count, KVH, per_group, HD)
    cache_keys = kv_cache[:, :, :kv_width].reshape(row_count, -1, KVH, HD)
    cache_values = kv_cache[:, :, kv_width:].reshape(row_count, -1, KVH, HD)
    cache_len = cache_keys.shape[1]
    scores = (
        jnp.einsum(
            "rskgd,rckd->rskgc", grouped_query, cache_keys, preferred_element_type=jnp.float32
        )
        * score_scale
    )
    positions = tensor_place * cache_len + jnp.arange(cache_len, dtype=jnp.int32)
    usable = (positions[None, :] < lengths[:, None])[:, None, None, None, :]
    block_peak = jnp.max(jnp.where(usable, scores, NEGATIVE), axis=-1)
    weights = jnp.where(usable, jnp.exp(scores - block_peak[..., None]), 0.0)
    weight_total = jnp.sum(weights, axis=-1)
    weighted = jnp.einsum(
        "rskgc,rckd->rskgd",
        weights.astype(jnp.bfloat16),
        cache_values,
        preferred_element_type=jnp.float32,
    )
    heads_own = H // tensor_count
    head_start = tensor_place * heads_own
    peak_all, total_all, sum_all = joined_2((block_peak, weight_total, weighted), "tensor", combine)
    peak_own = lax.dynamic_slice_in_dim(
        peak_all.reshape(row_count, step_count, H), head_start, heads_own, 2
    )
    total_own = lax.dynamic_slice_in_dim(
        total_all.reshape(row_count, step_count, H), head_start, heads_own, 2
    )
    sum_own = lax.dynamic_slice_in_dim(
        sum_all.reshape(row_count, step_count, H, HD), head_start, heads_own, 2
    )
    head_ids = head_start + jnp.arange(heads_own, dtype=jnp.int32)
    selector = (head_ids[:, None] // per_group == jnp.arange(KVH, dtype=jnp.int32)[None, :]).astype(
        jnp.bfloat16
    )
    appended = new_all.reshape(row_count, step_count, 2, KVH, HD)
    own_keys = jnp.einsum(
        "rtkd,hk->rthd", appended[:, :, 0], selector, preferred_element_type=jnp.float32
    ).astype(jnp.bfloat16)
    own_values = jnp.einsum(
        "rtkd,hk->rthd", appended[:, :, 1], selector, preferred_element_type=jnp.float32
    ).astype(jnp.bfloat16)
    own_query = lax.dynamic_slice_in_dim(
        queries.reshape(row_count, step_count, H, HD), head_start, heads_own, 2
    )
    near_scores = (
        jnp.einsum("rshd,rthd->rsht", own_query, own_keys, preferred_element_type=jnp.float32)
        * score_scale
    )
    causal = (jnp.arange(step_count)[:, None] >= jnp.arange(step_count)[None, :])[None, :, None, :]
    near_peak = jnp.max(jnp.where(causal, near_scores, NEGATIVE), axis=-1)
    near_weights = jnp.where(causal, jnp.exp(near_scores - near_peak[..., None]), 0.0)
    near_total = jnp.sum(near_weights, axis=-1)
    near_sum = jnp.einsum(
        "rsht,rthd->rshd",
        near_weights.astype(jnp.bfloat16),
        own_values,
        preferred_element_type=jnp.float32,
    )
    joined_peak = jnp.maximum(peak_own, near_peak)
    cache_scale = jnp.exp(peak_own - joined_peak)
    near_scale = jnp.exp(near_peak - joined_peak)
    numerator = sum_own * cache_scale[..., None] + near_sum * near_scale[..., None]
    denominator = total_own * cache_scale + near_total * near_scale
    attended = (
        (numerator / denominator[..., None])
        .astype(jnp.bfloat16)
        .reshape(row_count, step_count, heads_own * HD)
    )
    return (new_out, attended)


def solution(mesh):
    in_specs = (
        P("group", None, "tensor"),
        P(None, "tensor"),
        P("group", "tensor"),
        P("group", "tensor"),
        P(),
        P("group", "tensor", None),
        P("group", None, None),
        P("group"),
    )
    out_specs = (P("group", None, "tensor"), P("group", None, "tensor"))
    return jax.shard_map(
        on_device, mesh=mesh, in_specs=in_specs, out_specs=out_specs, check_vma=False
    )
```

profile of v0, /device:TPU:2, one launch (start us, length us, event | category | flops | bytes accessed | tf_op | source)
XLA Modules:
  0.0 293.6 jit_solution(14354292844045632534)
XLA Ops:
  8.0 2.8 fusion.48
  10.8 2.3 copy.79
  14.5 1.7 select_reduce_fusion
  18.1 52.7 %all-gather.1 = f32[32,8,8,8]{3,2,1,0:T(8,128)S(1)} all-gather(f32[2,8,8,8]{3,2,1,0:T(8,128)S(1)} %copy.56), channel_id=3, replica_groups=mesh['group'=32,'tensor'=16] {'tensor'}, dimensions={0}, use_global_device_ids=true | all-gather | bytes 69632 | tf_op jit(solution)/shard_map/all_gather | solution.py:15
  71.8 48.8 %all-gather = f32[32,8,8,8]{3,2,1,0:T(8,128)S(1)} all-gather(f32[2,8,8,8]{3,2,1,0:T(8,128)S(1)} %copy.55), channel_id=2, replica_groups=mesh['group'=32,'tensor'=16] {'tensor'}, dimensions={0}, use_global_device_ids=true | all-gather | bytes 69632 | tf_op jit(solution)/shard_map/all_gather | solution.py:15
  121.6 40.8 %all-gather.3 = bf16[32,64,4]{1,2,0:T(4,128)(2,1)S(1)} all-gather(bf16[1,64,4]{1,2,0:T(4,128)(2,1)S(1)} %bitcast.113), channel_id=1, replica_groups=mesh['group'=32,'tensor'=16] {'group'}, dimensions={0}, use_global_device_ids=true | all-gather | bytes 16896 | tf_op jit(solution)/shard_map/all_gather | solution.py:61
  162.9 4.7 %mul.132 = f32[2048,4,128]{2,1,0:T(4,128)S(1)} broadcast(f32[2048,4]{1,0:T(8,128)S(1)} %bitcast.100), dimensions={0,1} | broadcast | bytes 4227072 | tf_op jit(solution)/shard_map/mul | solution.py:28
  169.4 76.9 %all-reduce.1 = bf16[16,2048]{1,0:T(8,128)(2,1)S(1)} all-reduce(f32[16,2048]{1,0:T(8,128)S(1)} %convolution_add_fusion), channel_id=1, replica_groups=mesh['group'=32,'tensor'=16] {'tensor'}, use_global_device_ids=true, to_apply=%region_0.0 | all-reduce | flops 32768 | bytes 196608 | tf_op jit(solution)/shard_map/psum | solution.py:79
  249.3 36.1 %while.19 = (s32[]{:T(128)}, f32[2,8,8,8]{3,2,1,0:T(8,128)S(1)}, f32[2,8,8,8]{3,2,1,0:T(8,128)S(1)}, f32[2,8,8,8,128]{4,3,2,1,0:T(8,128)S(1)}, f32[16,2,8,8,8]{4...) while((s32[]{:T(128)}, f32[2,8,8,8]{3,2,1,0:T(8,128)S(1)}, ...), condition=%wide.region_4.5_spmd, body=%wide.region_3.4_spmd.sunk | while | flops 399365 | bytes 1613975 | solution.py:21
  250.3 1.4 fusion.57
  252.7 1.4 fusion.57
  255.1 1.4 fusion.57
  257.5 1.4 fusion.57
  259.9 1.4 fusion.57
  262.3 1.4 fusion.57
  264.7 1.4 fusion.57
  267.2 1.4 fusion.57
  269.6 1.4 fusion.57
  272.0 1.4 fusion.57
  274.4 1.4 fusion.57
  276.8 1.4 fusion.57
  279.2 1.4 fusion.57
  281.6 1.4 fusion.57
  284.0 1.4 fusion.57
  (72 shorter events, 26.7 us)
Async XLA Ops:
  7.2 161.6 %copy-start = (bf16[2048,512]{1,0:T(8,128)(2,1)S(1)}, bf16[2048,512]{1,0:T(8,128)(2,1)}, u32[]{:S(2)}) copy-start(bf16[2048,512]{1,0:T(8,128)(2,1)} %param.11) | copy-start | bytes 6291460
  7.2 155.7 %all-gather.7.cloned.1.call-start = ((), (), s32[]{:S(2)}) async-start(), calls=%async_computation | async-start | bytes 2162688 | tf_op jit(solution)/shard_map/all_gather | solution.py:60
  7.9 240.3 %all-gather.9.cloned.1.call-start = ((), (), s32[]{:S(2)}) async-start(), calls=%async_computation.1 | async-start | bytes 8912896 | tf_op jit(solution)/shard_map/all_gather | solution.py:15
  10.8 3.6 %copy-start.9 = (s32[2]{0:T(128)S(1)}, s32[2]{0:T(128)}, u32[]{:S(2)}) copy-start(s32[2]{0:T(128)} %param.17) | copy-start | bytes 28
  10.8 3.7 %copy-start.6 = (bf16[2,8,8192]{2,1,0:T(8,128)(2,1)S(1)}, bf16[2,8,8192]{2,1,0:T(8,128)(2,1)}, u32[]{:S(2)}) copy-start(bf16[2,8,8192]{2,1,0:T(8,128)(2,1)} %param.16) | copy-start | bytes 786436
  14.4 1.8 copy-start.1
  17.6 103.9 %copy-start.7 = (bf16[64,4]{0,1:T(4,128)(2,1)S(1)}, bf16[64,4]{0,1:T(4,128)(2,1)}, u32[]{:S(2)}) copy-start(bf16[64,4]{0,1:T(4,128)(2,1)} %param.13) | copy-start | bytes 1540
  70.8 1.0 copy-start.3
  120.6 1.0 copy-start.4
  162.9 4.7 %copy-start.2 = (bf16[2048,512]{1,0:T(8,128)(2,1)S(1)}, bf16[2048,512]{1,0:T(8,128)(2,1)}, u32[]{:S(2)}) copy-start(bf16[2048,512]{1,0:T(8,128)(2,1)} %all-gather.7.cloned.1.call-done) | copy-start | bytes 6291460
  162.9 4.7 %copy-start.5 = (bf16[2,8,512]{2,1,0:T(8,128)(2,1)S(1)}, bf16[2,8,512]{2,1,0:T(8,128)(2,1)}, u32[]{:S(2)}) copy-start(bf16[2,8,512]{2,1,0:T(8,128)(2,1)} %param.10) | copy-start | bytes 49156
  167.6 0.8 copy-start.8
Sparse Core Ops, SparseCore 0:
  10.2 72.2 all-gather.6
  85.6 144.1 all-gather.8
where the time goes:
time: 295 us; the launch traced here: 294 us
  blocking collectives  219 us (74%)
  other arithmetic  36.3 us (12%)
  local copies, waits for them, and re-layouts  16.9 us (6%)
  between operations  14.2 us (5%)
  matrix products  5.83 us (2%)
    all_gather x2, blocking collectives, joined_2(): everything = jax.tree.map(lambda part: lax.all_gather(part, axis), x)  101 us
    psum x1, blocking collectives, on_device(): summed = lax.psum(base_part + ordered, 'tensor')  76.9 us
    all_gather x1, blocking collectives, on_device(): lax.all_gather(delta_scales, 'group', axis=0, tiled=True)  40.8 us
    add x15, other arithmetic, combine(): left_sum * left_scale[..., None] + right_sum * right_scale[..., None]  21.6 us
    add x15, other arithmetic, combine(): left_total * left_scale + right_total * right_scale  14.1 us
  transfers between devices with their start and end apart: 2, of which 0 were waited for; matrix products, arithmetic and copies ran while one was open for 6% of the time, Pallas kernels for 0%

commit v1 on v0

v1 whole, which is shorter than its diff:
```python
import functools

import jax
import jax.numpy as jnp
from jax import lax
from jax.experimental import pallas as pl
from jax.experimental.pallas import tpu as pltpu
from jax.sharding import PartitionSpec as P

HD = 128
NEGATIVE = -1e30
MESH = pl.DeviceIdType.MESH
F32 = jnp.float32
BF16 = jnp.bfloat16


def nt_dot(a, b):
    return lax.dot_general(a, b, (((1,), (1,)), ((), ())), preferred_element_type=F32)


def kernel(
    NG,
    NT,
    hid_hbm,
    base_hbm,
    codes_hbm,
    scales_ref,
    owner_ref,
    cache_hbm,
    query_hbm,
    lengths_ref,
    new_ref,
    att_ref,
    hid,
    base,
    codes,
    cache,
    query,
    weight,
    place,
    back_send,
    back,
    proj_send,
    proj,
    part_send,
    part,
    lse_cols,
    lse_send,
    lse,
    pair_send,
    pair,
    load_sem,
    hid_send_sem,
    hid_sem,
    weight_send_sem,
    weight_sem,
    back_send_sem,
    back_sem,
    proj_send_sem,
    proj_sem,
    part_send_sem,
    part_sem,
    lse_send_sem,
    lse_sem,
    pair_send_sem,
    pair_sem,
):
    NZ = NG // 4
    KVH = NT // 2
    POS = cache.shape[0] // 2
    KVW = KVH * HD
    scale = HD ** (-0.5)
    me_g = lax.axis_index("group")
    me_t = lax.axis_index("tensor")
    core = lax.rem(me_g, 2)
    me_z = lax.rem(me_g // 2, NZ)
    x_lo = me_g // (2 * NZ)
    me_m = x_lo * 2 + core

    def group_of(m, z):
        return (m // 2) * (2 * NZ) + z * 2 + lax.rem(m, 2)

    def z_peer(i):
        return lax.rem(me_z + i, NZ)

    def m_peer(i):
        return lax.rem(me_m + i, 4)

    def t_peer(i):
        return lax.rem(me_t + i, NT)

    barrier = pltpu.get_barrier_semaphore()

    def greet_z(i, c):
        pl.semaphore_signal(
            barrier, inc=1, device_id=(group_of(me_m, z_peer(i)), me_t), device_id_type=MESH
        )
        return c

    def greet_m(i, c):
        pl.semaphore_signal(
            barrier, inc=1, device_id=(group_of(m_peer(i), me_z), me_t), device_id_type=MESH
        )
        return c

    def greet_t(i, c):
        pl.semaphore_signal(barrier, inc=1, device_id=(me_g, t_peer(i)), device_id_type=MESH)
        return c

    lax.fori_loop(1, NZ, greet_z, 0)
    lax.fori_loop(1, 4, greet_m, 0)
    lax.fori_loop(1, NT, greet_t, 0)

    loads = [
        pltpu.make_async_copy(codes_hbm, codes, load_sem.at[0]),
        pltpu.make_async_copy(hid_hbm, hid.at[me_z], load_sem.at[1]),
        pltpu.make_async_copy(query_hbm, query, load_sem.at[2]),
        pltpu.make_async_copy(cache_hbm.at[pl.ds(0, POS)], cache.at[pl.ds(0, POS)], load_sem.at[3]),
        pltpu.make_async_copy(
            cache_hbm.at[pl.ds(POS, POS)], cache.at[pl.ds(POS, POS)], load_sem.at[4]
        ),
        pltpu.make_async_copy(base_hbm, base, load_sem.at[5]),
    ]
    for load in loads:
        load.start()

    row = lax.broadcasted_iota(jnp.int32, (64, 64), 0)
    col = lax.broadcasted_iota(jnp.int32, (64, 64), 1)
    unit = (row == col).astype(BF16)
    scale_cols = nt_dot(unit, scales_ref[...])
    loads[0].wait()
    blocks = codes.shape[1] // 128
    own_weight = jnp.concatenate(
        [
            codes[:, j * 128 : (j + 1) * 128].astype(F32) * scale_cols[:, j : j + 1]
            for j in range(blocks)
        ],
        axis=1,
    ).astype(BF16)
    weight[me_m] = own_weight
    loads[1].wait()

    pl.semaphore_wait(barrier, (NZ - 1) + 3 + (NT - 1))

    def hid_copy(i):
        return pltpu.make_async_remote_copy(
            src_ref=hid.at[me_z],
            dst_ref=hid.at[me_z],
            send_sem=hid_send_sem.at[i],
            recv_sem=hid_sem.at[me_z],
            device_id=(group_of(me_m, z_peer(i)), me_t),
            device_id_type=MESH,
        )

    def weight_copy(i):
        return pltpu.make_async_remote_copy(
            src_ref=weight.at[me_m],
            dst_ref=weight.at[me_m],
            send_sem=weight_send_sem.at[i],
            recv_sem=weight_sem.at[me_m],
            device_id=(group_of(m_peer(i), me_z), me_t),
            device_id_type=MESH,
        )

    def start_hid(i, c):
        hid_copy(i).start()
        return c

    def start_weight(i, c):
        weight_copy(i).start()
        return c

    lax.fori_loop(1, NZ, start_hid, 0)
    lax.fori_loop(1, 4, start_weight, 0)

    def find(b, c):
        spot = jnp.int32(0)
        for g in range(NG):
            at = ((g // 2) % NZ) * 4 + (g // (2 * NZ)) * 2 + g % 2
            spot = jnp.where(owner_ref[g] == b, jnp.int32(at), spot)
        place[b] = spot
        return c

    lax.fori_loop(0, NG, find, 0)

    for load in loads[2:5]:
        load.wait()
    lse_cols[...] = jnp.zeros_like(lse_cols)
    lane = lax.broadcasted_iota(jnp.int32, (32, 128), 1)
    position = me_t * POS + lax.broadcasted_iota(jnp.int32, (64, POS), 1)

    def part_copy(dest, i):
        return pltpu.make_async_remote_copy(
            src_ref=part_send.at[dest],
            dst_ref=part.at[me_t],
            send_sem=part_send_sem.at[dest],
            recv_sem=part_sem.at[me_t],
            device_id=(me_g, dest),
            device_id_type=MESH,
        )

    def cached(i, c):
        k = lax.rem(me_t // 2 + 1 + i, KVH)
        q_both = query[:, pl.ds(pl.multiple_of(k * 1024, 1024), 1024)].astype(F32)
        for r in range(2):
            q = jnp.concatenate(
                [q_both[r * 8 : (r + 1) * 8, h * HD : (h + 1) * HD] for h in range(8)], axis=0
            ).astype(BF16)
            keys = cache[r * POS : (r + 1) * POS, pl.ds(pl.multiple_of(k * HD, HD), HD)]
            values = cache[r * POS : (r + 1) * POS, pl.ds(pl.multiple_of(KVW + k * HD, HD), HD)]
            scores = nt_dot(q, keys) * scale
            usable = position < lengths_ref[r]
            peak = jnp.max(jnp.where(usable, scores, NEGATIVE), axis=1, keepdims=True)
            weights = jnp.where(usable, jnp.exp(scores - peak), 0.0)
            total = jnp.sum(weights, axis=1, keepdims=True)
            weighted = jnp.dot(weights.astype(BF16), values, preferred_element_type=F32)
            some = total > 0.0
            safe = jnp.where(some, total, 1.0)
            mean = (weighted / safe).astype(BF16)
            log_sum = jnp.where(some, peak + jnp.log(safe), NEGATIVE)
            for half in range(2):
                dest = 2 * k + half
                part_send[dest, r * 32 : (r + 1) * 32] = mean[half * 32 : (half + 1) * 32]
                lse_cols[0:32] = jnp.where(
                    lane == dest * 8 + r, log_sum[half * 32 : (half + 1) * 32], lse_cols[0:32]
                )
        for half in range(2):
            dest = 2 * k + half

            @pl.when(dest != me_t)
            def _():
                part_copy(dest, i).start()

            @pl.when(dest == me_t)
            def _():
                part[me_t] = part_send[dest]

        return c

    lax.fori_loop(0, KVH, cached, 0)

    lse_send[...] = lse_cols[...].T[: NT * 8].reshape(lse_send.shape)

    def lse_copy(i):
        dest = t_peer(i)
        return pltpu.make_async_remote_copy(
            src_ref=lse_send.at[dest],
            dst_ref=lse.at[me_t],
            send_sem=lse_send_sem.at[i],
            recv_sem=lse_sem.at[me_t],
            device_id=(me_g, dest),
            device_id_type=MESH,
        )

    def start_lse(i, c):
        lse_copy(i).start()
        return c

    lax.fori_loop(1, NT, start_lse, 0)
    lse[me_t] = lse_send[me_t]

    def wait_hid(i, c):
        z = z_peer(i)
        pltpu.make_async_remote_copy(
            src_ref=hid.at[z],
            dst_ref=hid.at[z],
            send_sem=hid_send_sem.at[i],
            recv_sem=hid_sem.at[z],
            device_id=(group_of(me_m, z), me_t),
            device_id_type=MESH,
        ).wait_recv()
        return c

    def wait_weight(i, c):
        m = m_peer(i)
        pltpu.make_async_remote_copy(
            src_ref=weight.at[m],
            dst_ref=weight.at[m],
            send_sem=weight_send_sem.at[i],
            recv_sem=weight_sem.at[m],
            device_id=(group_of(m, me_z), me_t),
            device_id_type=MESH,
        ).wait_recv()
        return c

    lax.fori_loop(1, NZ, wait_hid, 0)
    lax.fori_loop(1, 4, wait_weight, 0)
    width = hid.shape[2]
    product = nt_dot(
        hid[...].reshape(NZ * 16, width), weight[...].reshape(4 * 64, width)
    ).reshape(NZ, 2, 8, 256)
    low = lax.broadcasted_iota(jnp.int32, (NZ, 8, 128), 2) < 64
    back_both = back_send
    for j in range(2):
        first = product[:, 0, :, j * 128 : (j + 1) * 128]
        second = product[:, 1, :, j * 128 : (j + 1) * 128]
        even = jnp.where(low, first, pltpu.roll(second, 64, 2))
        odd = jnp.where(low, pltpu.roll(first, 64, 2), second)
        back_both[:, 2 * j] = even
        back_both[:, 2 * j + 1] = odd

    def back_copy(i):
        z = z_peer(i)
        return pltpu.make_async_remote_copy(
            src_ref=back_send.at[z],
            dst_ref=back.at[pl.ds(me_z * 4, 4)],
            send_sem=back_send_sem.at[i],
            recv_sem=back_sem.at[me_z],
            device_id=(group_of(me_m, z), me_t),
            device_id_type=MESH,
        )

    def start_back(i, c):
        back_copy(i).start()
        return c

    lax.fori_loop(1, NZ, start_back, 0)
    back[pl.ds(me_z * 4, 4)] = back_send[me_z]

    loads[5].wait()
    own_rows = hid[me_z]

    def base_tile(j, c):
        rows = base[pl.ds(pl.multiple_of(j * 256, 256), 256), :]
        tile = nt_dot(own_rows, rows)
        proj_send[2 * j] = tile[:, :128]
        proj_send[2 * j + 1] = tile[:, 128:]
        return c

    lax.fori_loop(0, NT // 2, base_tile, 0)

    def wait_back(i, c):
        z = z_peer(i)
        pltpu.make_async_remote_copy(
            src_ref=back_send.at[z],
            dst_ref=back.at[pl.ds(z * 4, 4)],
            send_sem=back_send_sem.at[i],
            recv_sem=back_sem.at[z],
            device_id=(group_of(me_m, z), me_t),
            device_id_type=MESH,
        ).wait_recv()
        return c

    lax.fori_loop(1, NZ, wait_back, 0)
    low8 = lax.broadcasted_iota(jnp.int32, (8, 128), 1) < 64

    def proj_copy(i):
        dest = t_peer(i)
        return pltpu.make_async_remote_copy(
            src_ref=proj_send.at[dest],
            dst_ref=proj.at[me_t],
            send_sem=proj_send_sem.at[i],
            recv_sem=proj_sem.at[me_t],
            device_id=(me_g, dest),
            device_id_type=MESH,
        )

    def whole(dest):
        a = back[place[2 * dest]]
        b = back[place[2 * dest + 1]]
        first = jnp.where(low8, a, pltpu.roll(b, 64, 1))
        second = jnp.where(low8, pltpu.roll(a, 64, 1), b)
        return proj_send[dest] + jnp.concatenate([first, second], axis=0)

    def start_proj(i, c):
        dest = t_peer(i)
        proj_send[dest] = whole(dest)
        proj_copy(i).start()
        return c

    lax.fori_loop(1, NT, start_proj, 0)
    proj[me_t] = whole(me_t)

    def wait_part(i, c):
        u = t_peer(i)
        pltpu.make_async_remote_copy(
            src_ref=lse_send.at[u],
            dst_ref=lse.at[u],
            send_sem=lse_send_sem.at[i],
            recv_sem=lse_sem.at[u],
            device_id=(me_g, u),
            device_id_type=MESH,
        ).wait_recv()
        pltpu.make_async_remote_copy(
            src_ref=part_send.at[u],
            dst_ref=part.at[u],
            send_sem=part_send_sem.at[u],
            recv_sem=part_sem.at[u],
            device_id=(me_g, u),
            device_id_type=MESH,
        ).wait_recv()
        return c

    lax.fori_loop(1, NT, wait_part, 0)
    logs = lse[...]
    top = jnp.max(logs, axis=0)
    grown = jnp.exp(logs - top[None])
    sub = lax.broadcasted_iota(jnp.int32, (8, 128), 0)
    top_down = jnp.concatenate([top[0:2], top[0:2], top[0:4]], axis=0)
    with_top = jnp.where(sub < 2, grown[0], top_down)
    factors = jnp.concatenate([with_top[None], grown[1:]], axis=0).reshape(NT * 8, 128)
    if NT * 8 < 128:
        factors = jnp.concatenate([factors, jnp.zeros((128 - NT * 8, 128), F32)], axis=0)
    factors = factors.T[0:32]
    sums, totals, peaks = [], [], []
    for r in range(2):
        acc = jnp.zeros((32, HD), F32)
        total = jnp.zeros((32, 1), F32)
        for u in range(NT):
            factor = factors[:, u * 8 + r : u * 8 + r + 1]
            acc = acc + factor * part[u, r * 32 : (r + 1) * 32].astype(F32)
            total = total + factor
        sums.append(acc)
        totals.append(total)
        peaks.append(factors[:, 2 + r : 3 + r])
    cache_sum = jnp.concatenate(sums, axis=0)
    cache_total = jnp.concatenate(totals, axis=0)
    cache_peak = jnp.concatenate(peaks, axis=0)
    q_both = query[:, pl.ds(pl.multiple_of(me_t * 512, 512), 512)].astype(F32)
    q_own = jnp.concatenate(
        [
            q_both[r * 8 : (r + 1) * 8, h * HD : (h + 1) * HD]
            for r in range(2)
            for h in range(4)
        ],
        axis=0,
    ).astype(BF16)

    def wait_proj(i, c):
        u = t_peer(i)
        pltpu.make_async_remote_copy(
            src_ref=proj_send.at[u],
            dst_ref=proj.at[u],
            send_sem=proj_send_sem.at[i],
            recv_sem=proj_sem.at[u],
            device_id=(me_g, u),
            device_id_type=MESH,
        ).wait_recv()
        return c

    lax.fori_loop(1, NT, wait_proj, 0)
    fresh = jnp.sum(proj[...], axis=0).astype(BF16)
    pair_send[...] = fresh
    new_ref[...] = fresh
    is_value = me_t // KVH
    head = lax.rem(me_t, KVH)

    def pair_copy(half):
        return pltpu.make_async_remote_copy(
            src_ref=pair_send,
            dst_ref=pair.at[is_value],
            send_sem=pair_send_sem.at[half],
            recv_sem=pair_sem.at[is_value],
            device_id=(me_g, 2 * head + half),
            device_id_type=MESH,
        )

    for half in range(2):

        @pl.when(2 * head + half != me_t)
        def _():
            pair_copy(half).start()

        @pl.when(2 * head + half == me_t)
        def _():
            pair[is_value] = fresh

    for kind in range(2):
        source = kind * KVH + me_t // 2

        @pl.when(source != me_t)
        def _():
            pltpu.make_async_remote_copy(
                src_ref=pair_send,
                dst_ref=pair.at[kind],
                send_sem=pair_send_sem.at[kind],
                recv_sem=pair_sem.at[kind],
                device_id=(me_g, source),
                device_id_type=MESH,
            ).wait_recv()

    near = nt_dot(q_own, pair[0]) * scale
    at = lax.broadcasted_iota(jnp.int32, (64, 16), 0)
    to = lax.broadcasted_iota(jnp.int32, (64, 16), 1)
    causal = (at // 32 == to // 8) & (lax.rem(at, 8) >= lax.rem(to, 8))
    near_peak = jnp.max(jnp.where(causal, near, NEGATIVE), axis=1, keepdims=True)
    near_weights = jnp.where(causal, jnp.exp(near - near_peak), 0.0)
    near_total = jnp.sum(near_weights, axis=1, keepdims=True)
    near_sum = jnp.dot(near_weights.astype(BF16), pair[1], preferred_element_type=F32)
    joined = jnp.maximum(cache_peak, near_peak)
    cache_scale = jnp.exp(cache_peak - joined)
    near_scale = jnp.exp(near_peak - joined)
    numerator = cache_sum * cache_scale + near_sum * near_scale
    denominator = cache_total * cache_scale + near_total * near_scale
    result = numerator / denominator
    att_ref[...] = jnp.concatenate(
        [
            jnp.concatenate(
                [result[r * 32 + h * 8 : r * 32 + h * 8 + 8] for h in range(4)], axis=1
            )
            for r in range(2)
        ],
        axis=0,
    ).astype(BF16)

    def sent_z(i, c):
        hid_copy(i).wait_send()
        back_copy(i).wait_send()
        return c

    def sent_m(i, c):
        weight_copy(i).wait_send()
        return c

    def sent_t(i, c):
        lse_copy(i).wait_send()
        part_copy(t_peer(i), i).wait_send()
        proj_copy(i).wait_send()
        return c

    lax.fori_loop(1, NZ, sent_z, 0)
    lax.fori_loop(1, 4, sent_m, 0)
    lax.fori_loop(1, NT, sent_t, 0)
    for half in range(2):

        @pl.when(2 * head + half != me_t)
        def _():
            pair_copy(half).wait_send()


def on_device(
    hidden_x, base_weight, delta_codes, delta_scales, owner_map, kv_cache, queries, lengths
):
    NG = lax.axis_size("group")
    NT = lax.axis_size("tensor")
    NZ = NG // 4
    rows, steps, width = hidden_x.shape
    tokens = rows * steps
    positions = kv_cache.shape[1]
    any_space = pl.BlockSpec(memory_space=pltpu.HBM)
    vmem = pl.BlockSpec(memory_space=pltpu.VMEM)
    smem = pl.BlockSpec(memory_space=pltpu.SMEM)
    dma = pltpu.SemaphoreType.DMA
    new_kv, attended = pl.pallas_call(
        functools.partial(kernel, NG, NT),
        out_shape=(
            jax.ShapeDtypeStruct((tokens, 128), BF16),
            jax.ShapeDtypeStruct((tokens, 512), BF16),
        ),
        in_specs=[any_space, any_space, any_space, vmem, smem, any_space, any_space, smem],
        out_specs=(vmem, vmem),
        scratch_shapes=[
            pltpu.VMEM((NZ, tokens, width), BF16),
            pltpu.VMEM(base_weight.shape, BF16),
            pltpu.VMEM(delta_codes.shape, BF16),
            pltpu.VMEM((rows * positions, kv_cache.shape[2]), BF16),
            pltpu.VMEM((tokens, queries.shape[2]), BF16),
            pltpu.VMEM((4, 64, width), BF16),
            pltpu.SMEM((NG,), jnp.int32),
            pltpu.VMEM((NZ, 4, 8, 128), F32),
            pltpu.VMEM((NZ * 4, 8, 128), F32),
            pltpu.VMEM((NT, tokens, 128), F32),
            pltpu.VMEM((NT, tokens, 128), F32),
            pltpu.VMEM((NT, 64, HD), BF16),
            pltpu.VMEM((NT, 64, HD), BF16),
            pltpu.VMEM((128, 128), F32),
            pltpu.VMEM((NT, 8, 128), F32),
            pltpu.VMEM((NT, 8, 128), F32),
            pltpu.VMEM((tokens, 128), BF16),
            pltpu.VMEM((2, tokens, 128), BF16),
            dma((6,)),
            dma((NZ,)),
            dma((NZ,)),
            dma((4,)),
            dma((4,)),
            dma((NZ,)),
            dma((NZ,)),
            dma((NT,)),
            dma((NT,)),
            dma((NT,)),
            dma((NT,)),
            dma((NT,)),
            dma((NT,)),
            dma((2,)),
            dma((2,)),
        ],
        compiler_params=pltpu.CompilerParams(
            collective_id=0, has_side_effects=True, vmem_limit_bytes=60 * 1024 * 1024
        ),
    )(
        hidden_x.reshape(tokens, width),
        base_weight,
        delta_codes,
        delta_scales.T,
        owner_map,
        kv_cache.reshape(rows * positions, kv_cache.shape[2]),
        queries.reshape(tokens, queries.shape[2]),
        lengths,
    )
    return new_kv.reshape(rows, steps, 128), attended.reshape(rows, steps, 512)


def solution(mesh):
    in_specs = (
        P("group", None, "tensor"),
        P(None, "tensor"),
        P("group", "tensor"),
        P("group", "tensor"),
        P(),
        P("group", "tensor", None),
        P("group", None, None),
        P("group"),
    )
    out_specs = (P("group", None, "tensor"), P("group", None, "tensor"))
    return jax.shard_map(
        on_device, mesh=mesh, in_specs=in_specs, out_specs=out_specs, check_vma=False
    )
```

time: 295 us -> 45.8 us (0.16)
  the two profiles are of different devices: /device:TPU:2 before, /device:TPU:8 now
where the time goes in v1:
time: 45.8 us; the launch traced here: 45.6 us
  Pallas kernels  42.3 us (92%)
  local copies, waits for them, and re-layouts  2.59 us (6%)
  between operations  0.64 us (1%)
    pallas_call x1, Pallas kernels, on_device(): pl.pallas_call(functools.partial(kernel, NG, NT), out_shape=(jax.ShapeDty...  42.3 us
    unnamed x2, local copies, waits for them, and re-layouts  2.59 us

profile of v1, /device:TPU:8, one launch (start us, length us, event | category | flops | bytes accessed | tf_op | source)
XLA Modules:
  0.0 45.6 jit_solution(15702449433836584555)
XLA Ops:
  0.6 42.3 %shard_map.95 = (bf16[16,128]{1,0:T(8,128)(2,1)}, bf16[16,512]{1,0:T(8,128)(2,1)}) custom-call(bf16[16,512]{1,0:T(8,128)(2,1)} %bitcast.8, bf16[2048,512]{1,0:T(8,128)(2,1)} %base_hbm.1, bf16[64,512]{1,0:T(8,128)(2,1)} %codes_hbm.1, bf16[4,64]{1,0:T(4,128)(2,1)} %bitcast.11, s32[32]{0:T(128)} %owner_ref.1, bf16[512,2048]{1,0:T(8,128)(2,1)} %bitcast.6, ...), custom_call_target="tpu_custom_call" | custom-call | tf_op jit(solution)/shard_map/pallas_call | solution.py:544
  43.0 1.3 %copy.12 = bf16[2,8,128]{2,1,0:T(8,128)(2,1)} copy(bf16[2,8,128]{2,1,0:T(8,128)(2,1)} %bitcast.10) | data formatting | bytes 8192
  44.2 1.3 %copy.13 = bf16[2,8,512]{2,1,0:T(8,128)(2,1)} copy(bf16[2,8,512]{2,1,0:T(8,128)(2,1)} %bitcast.9) | data formatting | bytes 32768

commit v2 on v1

v2 whole, which is shorter than its diff:
```python
import functools

import jax
import jax.numpy as jnp
from jax import lax
from jax.experimental import pallas as pl
from jax.experimental.pallas import tpu as pltpu
from jax.sharding import PartitionSpec as P

HD = 128
NEGATIVE = -1e30
LOG2_E = 1.4426950408889634
MESH = pl.DeviceIdType.MESH
F32 = jnp.float32
BF16 = jnp.bfloat16


def nt_dot(a, b):
    return lax.dot_general(a, b, (((1,), (1,)), ((), ())), preferred_element_type=F32)


def kernel(
    NG,
    NT,
    hid_hbm,
    base_hbm,
    codes_hbm,
    scales_ref,
    owner_ref,
    cache_hbm,
    query_hbm,
    lengths_ref,
    fresh_ref,
    cached_ref,
    own_ref,
    hid,
    base,
    codes,
    cache,
    query,
    weight,
    place,
    back_send,
    back,
    base_proj,
    proj_send,
    proj,
    part_send,
    part,
    lse_cols,
    load_sem,
    hid_send_sem,
    hid_sem,
    weight_send_sem,
    weight_sem,
    back_send_sem,
    back_sem,
    proj_send_sem,
    proj_sem,
    part_send_sem,
    part_sem,
    ready_z,
    ready_t,
    ready_m,
):
    NZ = NG // 4
    NY = NT // 2
    KVH = NT // 2
    POS = cache.shape[0] // 2
    KVW = KVH * HD
    width = hid.shape[2]
    scale = HD ** (-0.5) * LOG2_E
    me_g = lax.axis_index("group")
    me_t = lax.axis_index("tensor")
    core = lax.rem(me_g, 2)
    me_z = lax.rem(me_g // 2, NZ)
    me_m = me_g // (2 * NZ) * 2 + core
    me_y = me_t // 2
    me_x = lax.rem(me_t, 2)

    def group_of(m, z):
        return (m // 2) * (2 * NZ) + z * 2 + lax.rem(m, 2)

    def near_peer(n):
        step = n // 2 + 1
        return lax.rem(me_z + jnp.where(lax.rem(n, 2) == 0, step, NZ - step), NZ)

    me_q = me_m + 1 - 2 * core

    def m_at(q):
        return q + 1 - 2 * lax.rem(q, 2)

    def t_peer(i):
        return lax.rem(me_t + i, NT)

    def order_of(t):
        y = t // 2
        near = jnp.where(y > NY // 2, 2 * (NY - y), jnp.maximum(2 * y - 1, 0))
        return near * 2 + lax.rem(t, 2)

    order = order_of(me_t)
    barrier = pltpu.get_barrier_semaphore()

    def greet_m(q, c):
        pl.semaphore_signal(
            barrier, inc=1, device_id=(group_of(m_at(q), me_z), me_t), device_id_type=MESH
        )
        return c

    def greet_z(z, c):
        pl.semaphore_signal(
            barrier, inc=1, device_id=(group_of(me_m, z), me_t), device_id_type=MESH
        )
        return c

    def greet_t(i, c):
        @pl.when(order_of(t_peer(i)) > order)
        def _():
            pl.semaphore_signal(
                barrier, inc=1, device_id=(me_g, t_peer(i)), device_id_type=MESH
            )

        return c

    def answer_z(z, c):
        pl.semaphore_signal(
            ready_z.at[me_z], inc=1, device_id=(group_of(me_m, z), me_t), device_id_type=MESH
        )
        return c

    def answer_m(q, c):
        pl.semaphore_signal(
            ready_m.at[me_q],
            inc=1,
            device_id=(group_of(m_at(q), me_z), me_t),
            device_id_type=MESH,
        )
        return c

    def answer_t(i, c):
        @pl.when(order_of(t_peer(i)) < order)
        def _():
            pl.semaphore_signal(ready_t, inc=1, device_id=(me_g, t_peer(i)), device_id_type=MESH)

        return c

    loads = [
        pltpu.make_async_copy(codes_hbm, codes, load_sem.at[0]),
        pltpu.make_async_copy(hid_hbm, hid.at[me_z], load_sem.at[1]),
        pltpu.make_async_copy(query_hbm, query, load_sem.at[2]),
        pltpu.make_async_copy(cache_hbm, cache, load_sem.at[3]),
        pltpu.make_async_copy(base_hbm, base, load_sem.at[4]),
    ]
    loads[0].start()
    loads[1].start()
    lax.fori_loop(me_q + 1, 4, greet_m, 0)
    lax.fori_loop(me_z + 1, NZ, greet_z, 0)
    lax.fori_loop(1, NT, greet_t, 0)
    for load in loads[2:]:
        load.start()

    unit = (
        lax.broadcasted_iota(jnp.int32, (64, 64), 0) == lax.broadcasted_iota(jnp.int32, (64, 64), 1)
    ).astype(BF16)
    scale_cols = nt_dot(unit, scales_ref[...])
    loads[0].wait()
    weight[me_m] = jnp.concatenate(
        [
            codes[:, j * 128 : (j + 1) * 128].astype(F32) * scale_cols[:, j : j + 1]
            for j in range(width // 128)
        ],
        axis=1,
    ).astype(BF16)
    loads[1].wait()

    def hid_copy(z):
        return pltpu.make_async_remote_copy(
            src_ref=hid.at[me_z],
            dst_ref=hid.at[me_z],
            send_sem=hid_send_sem.at[z],
            recv_sem=hid_sem.at[me_z],
            device_id=(group_of(me_m, z), me_t),
            device_id_type=MESH,
        )

    def wait_hid(z):
        pltpu.make_async_remote_copy(
            src_ref=hid.at[z],
            dst_ref=hid.at[z],
            send_sem=hid_send_sem.at[z],
            recv_sem=hid_sem.at[z],
            device_id=(group_of(me_m, z), me_t),
            device_id_type=MESH,
        ).wait_recv()

    def weight_copy(q):
        return pltpu.make_async_remote_copy(
            src_ref=weight.at[me_m],
            dst_ref=weight.at[me_m],
            send_sem=weight_send_sem.at[q],
            recv_sem=weight_sem.at[me_m],
            device_id=(group_of(m_at(q), me_z), me_t),
            device_id_type=MESH,
        )

    def start_weight_earlier(q, c):
        weight_copy(q).start()
        return c

    def start_weight_later(q, c):
        pl.semaphore_wait(ready_m.at[q], 1)
        weight_copy(q).start()
        return c

    def wait_weight(i, c):
        q = lax.rem(me_q + i, 4)
        m = m_at(q)
        pltpu.make_async_remote_copy(
            src_ref=weight.at[m],
            dst_ref=weight.at[m],
            send_sem=weight_send_sem.at[q],
            recv_sem=weight_sem.at[m],
            device_id=(group_of(m, me_z), me_t),
            device_id_type=MESH,
        ).wait_recv()
        return c

    def start_hid_earlier(n, c):
        @pl.when(near_peer(n) < me_z)
        def _():
            hid_copy(near_peer(n)).start()

        return c

    def start_hid_later(z, c):
        pl.semaphore_wait(ready_z.at[z], 1)
        hid_copy(z).start()
        return c

    @pl.when(me_z + order + me_q > 0)
    def _():
        pl.semaphore_wait(barrier, me_z + order + me_q)

    lax.fori_loop(0, me_q, answer_m, 0)
    lax.fori_loop(0, me_z, answer_z, 0)
    lax.fori_loop(0, me_q, start_weight_earlier, 0)
    lax.fori_loop(1, NT, answer_t, 0)
    lax.fori_loop(0, NZ - 1, start_hid_earlier, 0)
    lax.fori_loop(me_q + 1, 4, start_weight_later, 0)

    def back_copy(z):
        return pltpu.make_async_remote_copy(
            src_ref=back_send.at[z],
            dst_ref=back.at[pl.ds(me_z * 4, 4)],
            send_sem=back_send_sem.at[z],
            recv_sem=back_sem.at[me_z],
            device_id=(group_of(me_m, z), me_t),
            device_id_type=MESH,
        )

    def products(z):
        product = nt_dot(hid[z], weight[...].reshape(4 * 64, width))
        low = lax.broadcasted_iota(jnp.int32, (8, 128), 1) < 64
        for j in range(2):
            first = product[0:8, j * 128 : (j + 1) * 128]
            second = product[8:16, j * 128 : (j + 1) * 128]
            back_send[z, 2 * j] = jnp.where(low, first, pltpu.roll(second, 64, 1))
            back_send[z, 2 * j + 1] = jnp.where(low, pltpu.roll(first, 64, 1), second)

    def serve(z):
        wait_hid(z)
        products(z)
        back_copy(z).start()

    early_first = sorted(range(1, NZ), key=lambda d: min(d, NZ - d) + (d > NZ // 2) * 1.5)

    def serve_peer(n):
        step = jnp.int32(0)
        for place_in_list, d in enumerate(early_first):
            step = jnp.where(n == place_in_list, d, step)
        return lax.rem(me_z + step, NZ)

    def serve_earlier(n, c):
        @pl.when(serve_peer(n) < me_z)
        def _():
            serve(serve_peer(n))

        return c

    def serve_later(n, c):
        z = serve_peer(n)

        @pl.when((z > me_z) & (z < NZ - 1))
        def _():
            serve(z)

        return c

    last = me_z == NZ - 1

    def serve_first():
        lax.fori_loop(1, 4, wait_weight, 0)
        serve(0)

    def find(b):
        spot = jnp.int32(0)
        for g in range(NG):
            at = ((g // 2) % NZ) * 4 + (g // (2 * NZ)) * 2 + g % 2
            spot = jnp.where(owner_ref[g] == b, jnp.int32(at), spot)
        place[b] = spot

    lane = lax.broadcasted_iota(jnp.int32, (32, 128), 1)
    position = me_t * POS + lax.broadcasted_iota(jnp.int32, (64, POS), 1)
    own_rows = hid[me_z]
    for load in loads[2:]:
        load.wait()

    def cached(i, columns):
        for n in range(2):
            k = 2 * i + n
            q_both = query[:, pl.ds(pl.multiple_of(k * 1024, 1024), 1024)].astype(F32)
            for r in range(2):
                q = jnp.concatenate(
                    [q_both[r * 8 : (r + 1) * 8, h * HD : (h + 1) * HD] for h in range(8)], axis=0
                ).astype(BF16)
                keys = cache[r * POS : (r + 1) * POS, pl.ds(pl.multiple_of(k * HD, HD), HD)]
                values = cache[
                    r * POS : (r + 1) * POS, pl.ds(pl.multiple_of(KVW + k * HD, HD), HD)
                ]
                scores = jnp.where(position < lengths_ref[r], nt_dot(q, keys) * scale, NEGATIVE)
                peak = jnp.max(scores, axis=1, keepdims=True)
                weights = jnp.exp2(scores - peak)
                total = jnp.sum(weights, axis=1, keepdims=True)
                weighted = jnp.dot(weights.astype(BF16), values, preferred_element_type=F32)
                mean = (weighted * (1.0 / total)).astype(BF16)
                some = me_t * POS < lengths_ref[r]
                log_sum = jnp.where(some, peak + jnp.log2(total), NEGATIVE)
                for half in range(2):
                    dest = 2 * k + half
                    part_send[dest, r * 32 : (r + 1) * 32] = mean[half * 32 : (half + 1) * 32]
                    columns = jnp.where(
                        lane == dest * 8 + r, log_sum[half * 32 : (half + 1) * 32], columns
                    )
            rows = base[pl.ds(pl.multiple_of(k * 256, 256), 256), :]
            tile = nt_dot(own_rows, rows)
            base_proj[2 * k] = tile[:, :128]
            base_proj[2 * k + 1] = tile[:, 128:]
            for m in range(NG // KVH):
                find(k * (NG // KVH) + m)

        @pl.when(me_z + 1 + i < jnp.minimum(NZ - 1, me_z + KVH // 2))
        def _():
            start_hid_later(me_z + 1 + i, 0)

        @pl.when(last & (i == KVH // 2 - 2))
        def _():
            serve_first()

        return columns

    lse_cols[...] = jnp.zeros_like(lse_cols)
    lse_cols[0:32] = lax.fori_loop(0, KVH // 2, cached, jnp.zeros((32, 128), F32))

    def part_copy(i):
        dest = t_peer(i)
        return pltpu.make_async_remote_copy(
            src_ref=part_send.at[dest],
            dst_ref=part.at[me_t],
            send_sem=part_send_sem.at[i],
            recv_sem=part_sem.at[me_t],
            device_id=(me_g, dest),
            device_id_type=MESH,
        )

    def start_part(i, c):
        part_copy(i).start()
        return c

    def start_parts():
        logs = lse_cols[...].T[: NT * 8].reshape(NT, 8, 128)
        sub = lax.broadcasted_iota(jnp.int32, (NT, 8, 128), 1)
        high = logs.astype(BF16).astype(F32)
        rest = logs - high
        middle = rest.astype(BF16).astype(F32)
        low = rest - middle
        middle = jnp.concatenate([middle[:, 0:2], middle[:, 0:2], middle[:, 0:4]], axis=1)
        low = jnp.concatenate([low[:, 0:4], low[:, 0:2], low[:, 0:2]], axis=1)
        rows = jnp.where(sub < 2, high, jnp.where(sub < 4, middle, low))
        part_send[:, 64:80] = jnp.concatenate([rows, rows], axis=1).astype(BF16)

        @pl.when(order < NT - 1)
        def _():
            pl.semaphore_wait(ready_t, NT - 1 - order)

        lax.fori_loop(1, NT, start_part, 0)
        part[me_t] = part_send[me_t]

    @pl.when(me_z < NZ // 2)
    def _():
        start_parts()

    lax.fori_loop(me_z + KVH // 2, NZ - 1, start_hid_later, 0)

    @pl.when((me_z >= NZ // 2) & (me_z < NZ - 1))
    def _():
        start_hid_later(NZ - 1, 0)

    @pl.when(me_z >= NZ // 2)
    def _():
        start_parts()

    @pl.when(jnp.logical_not(last))
    def _():
        lax.fori_loop(1, 4, wait_weight, 0)

    lax.fori_loop(jnp.where(last, 1, 0), NZ - 1, serve_earlier, 0)

    @pl.when(me_z < NZ // 2)
    def _():
        start_hid_later(NZ - 1, 0)

    lax.fori_loop(0, NZ - 1, serve_later, 0)

    @pl.when(me_z < NZ - 1)
    def _():
        serve(NZ - 1)

    products(me_z)
    back[pl.ds(me_z * 4, 4)] = back_send[me_z]

    def wait_back(n, c):
        z = near_peer(n)
        pltpu.make_async_remote_copy(
            src_ref=back_send.at[z],
            dst_ref=back.at[pl.ds(z * 4, 4)],
            send_sem=back_send_sem.at[z],
            recv_sem=back_sem.at[z],
            device_id=(group_of(me_m, z), me_t),
            device_id_type=MESH,
        ).wait_recv()
        return c

    lax.fori_loop(0, NZ - 1, wait_back, 0)

    low8 = lax.broadcasted_iota(jnp.int32, (8, 128), 1) < 64

    def whole(block):
        a = back[place[2 * block]]
        b = back[place[2 * block + 1]]
        first = jnp.where(low8, a, pltpu.roll(b, 64, 1))
        second = jnp.where(low8, pltpu.roll(a, 64, 1), b)
        return base_proj[block] + jnp.concatenate([first, second], axis=0)

    def proj_copy(dest):
        return pltpu.make_async_remote_copy(
            src_ref=proj_send.at[dest],
            dst_ref=proj.at[me_t],
            send_sem=proj_send_sem.at[dest],
            recv_sem=proj_sem.at[me_t],
            device_id=(me_g, dest),
            device_id_type=MESH,
        )

    def far_y(n):
        step = (n + 1) // 2
        return lax.rem(me_y + NY // 2 + jnp.where(lax.rem(n, 2) == 0, step, NY - step), NY)

    def start_proj(n, c):
        y = far_y(n)
        key = whole(y)
        value = whole(KVH + y).astype(BF16)
        key_high = key.astype(BF16)
        key_low = (key - key_high.astype(F32)).astype(BF16)
        for x in range(2):
            dest = 2 * y + x
            proj_send[dest, 0:16] = key_high
            proj_send[dest, 16:32] = key_low
            proj_send[dest, 32:48] = value
            proj_send[dest, 48:64] = whole(dest).astype(BF16)
        proj_copy(2 * y + 1 - me_x).start()

        @pl.when(y != me_y)
        def _():
            proj_copy(2 * y + me_x).start()

        return c

    lax.fori_loop(0, NY, start_proj, 0)
    proj[me_t] = proj_send[me_t]

    def wait_part(i, c):
        u = t_peer(i)
        pltpu.make_async_remote_copy(
            src_ref=part_send.at[u],
            dst_ref=part.at[u],
            send_sem=part_send_sem.at[i],
            recv_sem=part_sem.at[u],
            device_id=(me_g, u),
            device_id_type=MESH,
        ).wait_recv()
        return c

    lax.fori_loop(1, NT, wait_part, 0)
    logs = part[:, 64:80].astype(F32)[:, 0:8]
    logs = (
        logs
        + jnp.concatenate([logs[:, 2:8], logs[:, 0:2]], axis=1)
        + jnp.concatenate([logs[:, 4:8], logs[:, 0:4]], axis=1)
    )
    top = jnp.max(logs, axis=0)
    grown = jnp.exp2(logs - top[None])
    sub = lax.broadcasted_iota(jnp.int32, (8, 128), 0)
    top_down = jnp.concatenate([top[0:2], top[0:2], top[0:4]], axis=0)
    with_top = jnp.where(sub < 2, grown[0], top_down)
    factors = jnp.concatenate([with_top[None], grown[1:]], axis=0).reshape(NT * 8, 128)
    if NT * 8 < 128:
        factors = jnp.concatenate([factors, jnp.zeros((128 - NT * 8, 128), F32)], axis=0)
    factors = factors.T[0:32]
    sums, totals, peaks = [], [], []
    for r in range(2):
        acc = jnp.zeros((32, HD), F32)
        total = jnp.zeros((32, 1), F32)
        for u in range(NT):
            factor = factors[:, u * 8 + r : u * 8 + r + 1]
            acc = acc + factor * part[u, r * 32 : (r + 1) * 32].astype(F32)
            total = total + factor
        sums.append(acc)
        totals.append(total)
        peaks.append(factors[:, 2 + r : 3 + r])
    cached_ref[:, 0:HD] = jnp.concatenate(sums, axis=0)
    half_lane = lax.broadcasted_iota(jnp.int32, (64, 128), 1) < 64
    cached_ref[:, HD : 2 * HD] = jnp.where(
        half_lane, jnp.concatenate(totals, axis=0), jnp.concatenate(peaks, axis=0)
    )
    q_both = query[:, pl.ds(pl.multiple_of(me_t * 512, 512), 512)].astype(F32)
    own_ref[...] = jnp.concatenate(
        [
            q_both[r * 8 : (r + 1) * 8, h * HD : (h + 1) * HD]
            for r in range(2)
            for h in range(4)
        ],
        axis=0,
    ).astype(BF16)

    def sent_z(n, c):
        hid_copy(near_peer(n)).wait_send()
        back_copy(near_peer(n)).wait_send()
        return c

    def sent_m(i, c):
        weight_copy(lax.rem(me_q + i, 4)).wait_send()
        return c

    def sent_t(i, c):
        part_copy(i).wait_send()
        proj_copy(t_peer(i)).wait_send()
        return c

    lax.fori_loop(0, NZ - 1, sent_z, 0)
    lax.fori_loop(1, 4, sent_m, 0)
    lax.fori_loop(1, NT, sent_t, 0)

    def wait_proj(i, c):
        u = t_peer(i)
        pltpu.make_async_remote_copy(
            src_ref=proj_send.at[u],
            dst_ref=proj.at[u],
            send_sem=proj_send_sem.at[u],
            recv_sem=proj_sem.at[u],
            device_id=(me_g, u),
            device_id_type=MESH,
        ).wait_recv()
        return c

    lax.fori_loop(1, NT, wait_proj, 0)
    summed = jnp.sum(proj[...].astype(F32), axis=0)
    fresh_ref[0] = (summed[0:16] + summed[16:32]).astype(BF16)
    fresh_ref[1] = summed[32:48].astype(BF16)
    fresh_ref[2] = summed[48:64].astype(BF16)


def finish(fresh_ref, cached_ref, own_ref, new_ref, att_ref):
    scale = HD ** (-0.5) * LOG2_E
    new_ref[...] = fresh_ref[2]
    cache_sum = cached_ref[:, 0:HD]
    cache_total = cached_ref[:, HD : HD + 1]
    cache_peak = cached_ref[:, HD + 64 : HD + 65]
    near = nt_dot(own_ref[...], fresh_ref[0]) * scale
    at = lax.broadcasted_iota(jnp.int32, (64, 16), 0)
    to = lax.broadcasted_iota(jnp.int32, (64, 16), 1)
    causal = (at // 32 == to // 8) & (lax.rem(at, 8) >= lax.rem(to, 8))
    near = jnp.where(causal, near, NEGATIVE)
    near_peak = jnp.max(near, axis=1, keepdims=True)
    near_weights = jnp.exp2(near - near_peak)
    near_total = jnp.sum(near_weights, axis=1, keepdims=True)
    near_sum = jnp.dot(near_weights.astype(BF16), fresh_ref[1], preferred_element_type=F32)
    joined = jnp.maximum(cache_peak, near_peak)
    cache_scale = jnp.exp2(cache_peak - joined)
    near_scale = jnp.exp2(near_peak - joined)
    numerator = cache_sum * cache_scale + near_sum * near_scale
    denominator = cache_total * cache_scale + near_total * near_scale
    result = numerator / denominator
    att_ref[...] = jnp.concatenate(
        [
            jnp.concatenate(
                [result[r * 32 + h * 8 : r * 32 + h * 8 + 8] for h in range(4)], axis=1
            )
            for r in range(2)
        ],
        axis=0,
    ).astype(BF16)


def on_device(
    hidden_x, base_weight, delta_codes, delta_scales, owner_map, kv_cache, queries, lengths
):
    NG = lax.axis_size("group")
    NT = lax.axis_size("tensor")
    NZ = NG // 4
    rows, steps, width = hidden_x.shape
    tokens = rows * steps
    positions = kv_cache.shape[1]
    any_space = pl.BlockSpec(memory_space=pl.ANY)
    vmem = pl.BlockSpec(memory_space=pltpu.VMEM)
    smem = pl.BlockSpec(memory_space=pltpu.SMEM)
    dma = pltpu.SemaphoreType.DMA
    fresh, cached, own_query = pl.pallas_call(
        functools.partial(kernel, NG, NT),
        out_shape=(
            jax.ShapeDtypeStruct((3, tokens, 128), BF16),
            jax.ShapeDtypeStruct((64, 256), F32),
            jax.ShapeDtypeStruct((64, 128), BF16),
        ),
        in_specs=[any_space, any_space, any_space, vmem, smem, any_space, any_space, smem],
        out_specs=(vmem, vmem, vmem),
        scratch_shapes=[
            pltpu.VMEM((NZ, tokens, width), BF16),
            pltpu.VMEM(base_weight.shape, BF16),
            pltpu.VMEM(delta_codes.shape, BF16),
            pltpu.VMEM((rows * positions, kv_cache.shape[2]), BF16),
            pltpu.VMEM((tokens, queries.shape[2]), BF16),
            pltpu.VMEM((4, 64, width), BF16),
            pltpu.SMEM((NG,), jnp.int32),
            pltpu.VMEM((NZ, 4, 8, 128), F32),
            pltpu.VMEM((NZ * 4, 8, 128), F32),
            pltpu.VMEM((NT, tokens, 128), F32),
            pltpu.VMEM((NT, 4 * tokens, 128), BF16),
            pltpu.VMEM((NT, 4 * tokens, 128), BF16),
            pltpu.VMEM((NT, 80, HD), BF16),
            pltpu.VMEM((NT, 80, HD), BF16),
            pltpu.VMEM((128, 128), F32),
            dma((5,)),
            dma((NZ,)),
            dma((NZ,)),
            dma((4,)),
            dma((4,)),
            dma((NZ,)),
            dma((NZ,)),
            dma((NT,)),
            dma((NT,)),
            dma((NT,)),
            dma((NT,)),
            pltpu.SemaphoreType.REGULAR((NZ,)),
            pltpu.SemaphoreType.REGULAR,
            pltpu.SemaphoreType.REGULAR((4,)),
        ],
        compiler_params=pltpu.CompilerParams(
            collective_id=0, has_side_effects=True, vmem_limit_bytes=60 * 1024 * 1024
        ),
    )(
        hidden_x.reshape(tokens, width),
        base_weight,
        delta_codes,
        delta_scales.T,
        owner_map,
        kv_cache.reshape(rows * positions, kv_cache.shape[2]),
        queries.reshape(tokens, queries.shape[2]),
        lengths,
    )
    new_kv, attended = pl.pallas_call(
        finish,
        out_shape=(
            jax.ShapeDtypeStruct((tokens, 128), BF16),
            jax.ShapeDtypeStruct((tokens, 512), BF16),
        ),
        in_specs=[vmem, vmem, vmem],
        out_specs=(vmem, vmem),
    )(fresh, cached, own_query)
    return new_kv.reshape(rows, steps, 128), attended.reshape(rows, steps, 512)


def solution(mesh):
    in_specs = (
        P("group", None, "tensor"),
        P(None, "tensor"),
        P("group", "tensor"),
        P("group", "tensor"),
        P(),
        P("group", "tensor", None),
        P("group", None, None),
        P("group"),
    )
    out_specs = (P("group", None, "tensor"), P("group", None, "tensor"))
    return jax.shard_map(
        on_device, mesh=mesh, in_specs=in_specs, out_specs=out_specs, check_vma=False
    )
```

time: 45.8 us -> 38.1 us (0.83)
  the two profiles are of different devices: /device:TPU:8 before, /device:TPU:6 now
where the time goes in v2:
time: 38.1 us; the launch traced here: 37.9 us
  Pallas kernels  37.3 us (98%)
  between operations  0.64 us (2%)
    pallas_call x1, Pallas kernels, on_device(): pl.pallas_call(functools.partial(kernel, NG, NT), out_shape=(jax.ShapeDty...  35.4 us
    pallas_call x1, Pallas kernels, on_device(): pl.pallas_call(finish, out_shape=(jax.ShapeDtypeStruct((tokens, 128), BF1...  1.89 us

profile of v2, /device:TPU:6, one launch (start us, length us, event | category | flops | bytes accessed | tf_op | source)
XLA Modules:
  0.0 37.9 jit_solution(9188605543346226453)
XLA Ops:
  0.6 35.4 %shard_map.95 = (bf16[3,16,128]{2,1,0:T(8,128)(2,1)}, f32[64,256]{1,0:T(8,128)}, bf16[64,128]{1,0:T(8,128)(2,1)}) custom-call(bf16[16,512]{1,0:T(8,128)(2,1)} %bitcast.8, bf16[2048,512]{1,0:T(8,128)(2,1)} %base_hbm.1, bf16[64,512]{1,0:T(8,128)(2,1)} %codes_hbm.1, bf16[4,64]{1,0:T(4,128)(2,1)} %bitcast.9, s32[32]{0:T(128)} %owner_ref.1, ...), custom_call_target="tpu_custom_call" | custom-call | tf_op jit(solution)/shard_map/pallas_call | solution.py:627
  36.0 1.9 %shard_map.96 = (bf16[16,128]{1,0:T(8,128)(2,1)}, bf16[16,512]{1,0:T(8,128)(2,1)}) custom-call(bf16[3,16,128]{2,1,0:T(8,128)(2,1)} %get-tuple-element.7.fresh_ref, f32[64,256]{1,0:T(8,128)} %get-tuple-element.8.cached_ref, bf16[64,128]{1,0:T(8,128)(2,1)} %get-tuple-element.9.own_ref), custom_call_target="tpu_custom_call" | custom-call | tf_op jit(solution)/shard_map/pallas_call | solution.py:680

commit v3 on v2

--- a/solution.py
+++ b/solution.py
@@ -61,6 +61,7 @@
     part_sem,
     ready_z,
     ready_t,
+    ready_x,
     ready_m,
 ):
     NZ = NG // 4
@@ -85,20 +86,18 @@
         step = n // 2 + 1
         return lax.rem(me_z + jnp.where(lax.rem(n, 2) == 0, step, NZ - step), NZ)
 
+    def t_peer(i):
+        return lax.rem(me_t + i, NT)
+
     me_q = me_m + 1 - 2 * core
 
     def m_at(q):
         return q + 1 - 2 * lax.rem(q, 2)
 
-    def t_peer(i):
-        return lax.rem(me_t + i, NT)
-
-    def order_of(t):
-        y = t // 2
-        near = jnp.where(y > NY // 2, 2 * (NY - y), jnp.maximum(2 * y - 1, 0))
-        return near * 2 + lax.rem(t, 2)
-
-    order = order_of(me_t)
+    last_y = NY // 2
+    at_last_y = me_y == last_y
+    herald = at_last_y & (me_x == 0)
+    greeted = me_z + me_q + jnp.where(at_last_y, NY - 1 + me_x, 0)
     barrier = pltpu.get_barrier_semaphore()
 
     def greet_m(q, c):
@@ -111,15 +110,6 @@
         pl.semaphore_signal(
             barrier, inc=1, device_id=(group_of(me_m, z), me_t), device_id_type=MESH
         )
-        return c
-
-    def greet_t(i, c):
-        @pl.when(order_of(t_peer(i)) > order)
-        def _():
-            pl.semaphore_signal(
-                barrier, inc=1, device_id=(me_g, t_peer(i)), device_id_type=MESH
-            )
-
         return c
 
     def answer_z(z, c):
@@ -155,9 +145,32 @@
     loads[1].start()
     lax.fori_loop(me_q + 1, 4, greet_m, 0)
     lax.fori_loop(me_z + 1, NZ, greet_z, 0)
-    lax.fori_loop(1, NT, greet_t, 0)
+
+    @pl.when(jnp.logical_not(at_last_y))
+    def _():
+        pl.semaphore_signal(
+            barrier, inc=1, device_id=(me_g, 2 * last_y + me_x), device_id_type=MESH
+        )
+
+    @pl.when(herald)
+    def _():
+        pl.semaphore_signal(
+            barrier, inc=1, device_id=(me_g, 2 * last_y + 1), device_id_type=MESH
+        )
+
     for load in loads[2:]:
         load.start()
+
+    @pl.when(greeted > 0)
+    def _():
+        pl.semaphore_wait(barrier, greeted)
+
+    lax.fori_loop(0, me_q, answer_m, 0)
+    lax.fori_loop(0, me_z, answer_z, 0)
+
+    @pl.when(at_last_y & (me_x == 1))
+    def _():
+        pl.semaphore_signal(ready_x, inc=1, device_id=(me_g, 2 * last_y), device_id_type=MESH)
 
     unit = (
         lax.broadcasted_iota(jnp.int32, (64, 64), 0) == lax.broadcasted_iota(jnp.int32, (64, 64), 1)
@@ -237,14 +250,8 @@
         hid_copy(z).start()
         return c
 
-    @pl.when(me_z + order + me_q > 0)
-    def _():
-        pl.semaphore_wait(barrier, me_z + order + me_q)
-
-    lax.fori_loop(0, me_q, answer_m, 0)
-    lax.fori_loop(0, me_z, answer_z, 0)
     lax.fori_loop(0, me_q, start_weight_earlier, 0)
-    lax.fori_loop(1, NT, answer_t, 0)
+
     lax.fori_loop(0, NZ - 1, start_hid_earlier, 0)
     lax.fori_loop(me_q + 1, 4, start_weight_later, 0)
 
@@ -352,11 +359,20 @@
         def _():
             start_hid_later(me_z + 1 + i, 0)
 
-        @pl.when(last & (i == KVH // 2 - 2))
+        @pl.when(last & (i == max(KVH // 2 - 3, 0)))
         def _():
             serve_first()
 
         return columns
+
+    def tell(i, c):
+        pl.semaphore_signal(ready_t, inc=1, device_id=(me_g, t_peer(i)), device_id_type=MESH)
+        return c
+
+    @pl.when(herald)
+    def _():
+        pl.semaphore_wait(ready_x, 1)
+        lax.fori_loop(1, NT, tell, 0)
 
     lse_cols[...] = jnp.zeros_like(lse_cols)
     lse_cols[0:32] = lax.fori_loop(0, KVH // 2, cached, jnp.zeros((32, 128), F32))
@@ -388,36 +404,46 @@
         rows = jnp.where(sub < 2, high, jnp.where(sub < 4, middle, low))
         part_send[:, 64:80] = jnp.concatenate([rows, rows], axis=1).astype(BF16)
 
-        @pl.when(order < NT - 1)
+        @pl.when(jnp.logical_not(herald))
         def _():
-            pl.semaphore_wait(ready_t, NT - 1 - order)
+            pl.semaphore_wait(ready_t, 1)
 
         lax.fori_loop(1, NT, start_part, 0)
         part[me_t] = part_send[me_t]
 
+    parts_first = (me_z < NZ // 2) & (jnp.abs(me_y - last_y) < 2)
+
+    @pl.when(parts_first)
+    def _():
+        start_parts()
+
+    lax.fori_loop(me_z + KVH // 2, NZ - 1, start_hid_later, 0)
+
+    @pl.when((me_z >= NZ // 2) & (me_z < NZ - 1))
+    def _():
+        start_hid_later(NZ - 1, 0)
+
+    @pl.when(last)
+    def _():
+        start_parts()
+
+    @pl.when(jnp.logical_not(last))
+    def _():
+        lax.fori_loop(1, 4, wait_weight, 0)
+
+    lax.fori_loop(jnp.where(last, 1, 0), NZ - 1, serve_earlier, 0)
+
+    @pl.when((me_z >= NZ // 2) & jnp.logical_not(last))
+    def _():
+        start_parts()
+
     @pl.when(me_z < NZ // 2)
     def _():
+        start_hid_later(NZ - 1, 0)
+
+    @pl.when((me_z < NZ // 2) & jnp.logical_not(parts_first))
+    def _():
         start_parts()
-
-    lax.fori_loop(me_z + KVH // 2, NZ - 1, start_hid_later, 0)
-
-    @pl.when((me_z >= NZ // 2) & (me_z < NZ - 1))
-    def _():
-        start_hid_later(NZ - 1, 0)
-
-    @pl.when(me_z >= NZ // 2)
-    def _():
-        start_parts()
-
-    @pl.when(jnp.logical_not(last))
-    def _():
-        lax.fori_loop(1, 4, wait_weight, 0)
-
-    lax.fori_loop(jnp.where(last, 1, 0), NZ - 1, serve_earlier, 0)
-
-    @pl.when(me_z < NZ // 2)
-    def _():
-        start_hid_later(NZ - 1, 0)
 
     lax.fori_loop(0, NZ - 1, serve_later, 0)
 
@@ -624,12 +650,16 @@
     vmem = pl.BlockSpec(memory_space=pltpu.VMEM)
     smem = pl.BlockSpec(memory_space=pltpu.SMEM)
     dma = pltpu.SemaphoreType.DMA
+
+    def in_hbm(x):
+        return pltpu.with_memory_space_constraint(x, pltpu.HBM)
+
     fresh, cached, own_query = pl.pallas_call(
         functools.partial(kernel, NG, NT),
         out_shape=(
-            jax.ShapeDtypeStruct((3, tokens, 128), BF16),
-            jax.ShapeDtypeStruct((64, 256), F32),
-            jax.ShapeDtypeStruct((64, 128), BF16),
+            pltpu.VMEM((3, tokens, 128), BF16),
+            pltpu.VMEM((64, 256), F32),
+            pltpu.VMEM((64, 128), BF16),
         ),
         in_specs=[any_space, any_space, any_space, vmem, smem, any_space, any_space, smem],
         out_specs=(vmem, vmem, vmem),
@@ -662,20 +692,21 @@
             dma((NT,)),
             pltpu.SemaphoreType.REGULAR((NZ,)),
             pltpu.SemaphoreType.REGULAR,
+            pltpu.SemaphoreType.REGULAR,
             pltpu.SemaphoreType.REGULAR((4,)),
         ],
         compiler_params=pltpu.CompilerParams(
-            collective_id=0, has_side_effects=True, vmem_limit_bytes=60 * 1024 * 1024
+            collective_id=0, has_side_effects=True, vmem_limit_bytes=48 * 1024 * 1024
         ),
     )(
-        hidden_x.reshape(tokens, width),
-        base_weight,
-        delta_codes,
-        delta_scales.T,
-        owner_map,
-        kv_cache.reshape(rows * positions, kv_cache.shape[2]),
-        queries.reshape(tokens, queries.shape[2]),
-        lengths,
+        in_hbm(hidden_x.reshape(tokens, width)),
+        in_hbm(base_weight),
+        in_hbm(delta_codes),
+        in_hbm(delta_scales.T),
+        in_hbm(owner_map),
+        in_hbm(kv_cache.reshape(rows * positions, kv_cache.shape[2])),
+        in_hbm(queries.reshape(tokens, queries.shape[2])),
+        in_hbm(lengths),
     )
     new_kv, attended = pl.pallas_call(
         finish,
@@ -685,6 +716,7 @@
         ),
         in_specs=[vmem, vmem, vmem],
         out_specs=(vmem, vmem),
+        compiler_params=pltpu.CompilerParams(vmem_limit_bytes=8 * 1024 * 1024),
     )(fresh, cached, own_query)
     return new_kv.reshape(rows, steps, 128), attended.reshape(rows, steps, 512)
 

time: 38.1 us -> 34.7 us (0.911)
  the two profiles are of different devices: /device:TPU:6 before, /device:TPU:8 now
where the time goes in v3:
time: 34.7 us; the launch traced here: 34.5 us
  Pallas kernels  33.9 us (98%)
  between operations  0.64 us (2%)
    pallas_call x1, Pallas kernels, on_device(): pl.pallas_call(functools.partial(kernel, NG, NT), out_shape=(pltpu.VMEM((...  32.8 us
    pallas_call x1, Pallas kernels, on_device(): pl.pallas_call(finish, out_shape=(jax.ShapeDtypeStruct((tokens, 128), BF1...  1.05 us

profile of v3, /device:TPU:8, one launch (start us, length us, event | category | flops | bytes accessed | tf_op | source)
XLA Modules:
  0.0 34.5 jit_solution(4051284663575471240)
XLA Ops:
  0.6 32.8 %shard_map.95 = (bf16[3,16,128]{2,1,0:T(8,128)(2,1)S(1)}, f32[64,256]{1,0:T(8,128)S(1)}, bf16[64,128]{1,0:T(8,128)(2,1)S(1)}) custom-call(bf16[16,512]{1,0:T(8,128)(2,1)} %bitcast.8, bf16[2048,512]{1,0:T(8,128)(2,1)} %base_hbm.1, bf16[64,512]{1,0:T(8,128)(2,1)} %codes_hbm.1, bf16[4,64]{1,0:T(4,128)(2,1)} %bitcast.9, s32[32]{0:T(128)} %owner_ref.1, ...), custom_call_target="tpu_custom_call" | custom-call | tf_op jit(solution)/shard_map/pallas_call | solution.py:657
  33.5 1.1 %shard_map.96 = (bf16[16,128]{1,0:T(8,128)(2,1)}, bf16[16,512]{1,0:T(8,128)(2,1)}) custom-call(bf16[3,16,128]{2,1,0:T(8,128)(2,1)S(1)} %get-tuple-element.7.fresh_ref, f32[64,256]{1,0:T(8,128)S(1)} %get-tuple-element.8.cached_ref, bf16[64,128]{1,0:T(8,128)(2,1)S(1)} %get-tuple-element.9.own_ref), custom_call_target="tpu_custom_call" | custom-call | tf_op jit(solution)/shard_map/pallas_call | solution.py:711

commit v4 on v3

--- a/solution.py
+++ b/solution.py
@@ -25,17 +25,20 @@
     hid_hbm,
     base_hbm,
     codes_hbm,
-    scales_ref,
-    owner_ref,
+    scales_hbm,
+    owner_hbm,
     cache_hbm,
     query_hbm,
-    lengths_ref,
+    lengths_hbm,
     fresh_ref,
     cached_ref,
     own_ref,
     hid,
     base,
     codes,
+    scales_ref,
+    owner_ref,
+    lengths_ref,
     cache,
     query,
     weight,
@@ -140,7 +143,11 @@
         pltpu.make_async_copy(query_hbm, query, load_sem.at[2]),
         pltpu.make_async_copy(cache_hbm, cache, load_sem.at[3]),
         pltpu.make_async_copy(base_hbm, base, load_sem.at[4]),
+        pltpu.make_async_copy(scales_hbm, scales_ref, load_sem.at[5]),
+        pltpu.make_async_copy(owner_hbm, owner_ref, load_sem.at[6]),
+        pltpu.make_async_copy(lengths_hbm, lengths_ref, load_sem.at[7]),
     ]
+    loads[5].start()
     loads[0].start()
     loads[1].start()
     lax.fori_loop(me_q + 1, 4, greet_m, 0)
@@ -158,7 +165,7 @@
             barrier, inc=1, device_id=(me_g, 2 * last_y + 1), device_id_type=MESH
         )
 
-    for load in loads[2:]:
+    for load in loads[2:5] + loads[6:]:
         load.start()
 
     @pl.when(greeted > 0)
@@ -175,6 +182,7 @@
     unit = (
         lax.broadcasted_iota(jnp.int32, (64, 64), 0) == lax.broadcasted_iota(jnp.int32, (64, 64), 1)
     ).astype(BF16)
+    loads[5].wait()
     scale_cols = nt_dot(unit, scales_ref[...])
     loads[0].wait()
     weight[me_m] = jnp.concatenate(
@@ -216,14 +224,12 @@
             device_id_type=MESH,
         )
 
-    def start_weight_earlier(q, c):
+    def start_weight(q):
+        @pl.when(q > me_q)
+        def _():
+            pl.semaphore_wait(ready_m.at[q], 1)
+
         weight_copy(q).start()
-        return c
-
-    def start_weight_later(q, c):
-        pl.semaphore_wait(ready_m.at[q], 1)
-        weight_copy(q).start()
-        return c
 
     def wait_weight(i, c):
         q = lax.rem(me_q + i, 4)
@@ -250,10 +256,11 @@
         hid_copy(z).start()
         return c
 
-    lax.fori_loop(0, me_q, start_weight_earlier, 0)
+    start_weight(lax.rem(me_q + 2, 4))
+    start_weight(3 - me_q)
+    start_weight(me_q + 1 - 2 * lax.rem(me_q, 2))
 
     lax.fori_loop(0, NZ - 1, start_hid_earlier, 0)
-    lax.fori_loop(me_q + 1, 4, start_weight_later, 0)
 
     def back_copy(z):
         return pltpu.make_async_remote_copy(
@@ -279,13 +286,8 @@
         products(z)
         back_copy(z).start()
 
-    early_first = sorted(range(1, NZ), key=lambda d: min(d, NZ - d) + (d > NZ // 2) * 1.5)
-
     def serve_peer(n):
-        step = jnp.int32(0)
-        for place_in_list, d in enumerate(early_first):
-            step = jnp.where(n == place_in_list, d, step)
-        return lax.rem(me_z + step, NZ)
+        return lax.rem(me_z + 1 + n, NZ)
 
     def serve_earlier(n, c):
         @pl.when(serve_peer(n) < me_z)
@@ -305,9 +307,7 @@
 
     last = me_z == NZ - 1
 
-    def serve_first():
-        lax.fori_loop(1, 4, wait_weight, 0)
-        serve(0)
+    between = KVH // 2 - 1
 
     def find(b):
         spot = jnp.int32(0)
@@ -319,7 +319,7 @@
     lane = lax.broadcasted_iota(jnp.int32, (32, 128), 1)
     position = me_t * POS + lax.broadcasted_iota(jnp.int32, (64, POS), 1)
     own_rows = hid[me_z]
-    for load in loads[2:]:
+    for load in loads[2:5] + loads[6:]:
         load.wait()
 
     def cached(i, columns):
@@ -359,9 +359,13 @@
         def _():
             start_hid_later(me_z + 1 + i, 0)
 
-        @pl.when(last & (i == max(KVH // 2 - 3, 0)))
-        def _():
-            serve_first()
+        @pl.when(last & (i == 1))
+        def _():
+            lax.fori_loop(1, 4, wait_weight, 0)
+
+        @pl.when(last & (i >= 1))
+        def _():
+            serve(i - 1)
 
         return columns
 
@@ -423,15 +427,16 @@
     def _():
         start_hid_later(NZ - 1, 0)
 
+    @pl.when(jnp.logical_not(last) | (between == 0))
+    def _():
+        lax.fori_loop(1, 4, wait_weight, 0)
+
     @pl.when(last)
     def _():
+        serve(between)
         start_parts()
 
-    @pl.when(jnp.logical_not(last))
-    def _():
-        lax.fori_loop(1, 4, wait_weight, 0)
-
-    lax.fori_loop(jnp.where(last, 1, 0), NZ - 1, serve_earlier, 0)
+    lax.fori_loop(jnp.where(last, between + 1, 0), NZ - 1, serve_earlier, 0)
 
     @pl.when((me_z >= NZ // 2) & jnp.logical_not(last))
     def _():
@@ -648,7 +653,6 @@
     positions = kv_cache.shape[1]
     any_space = pl.BlockSpec(memory_space=pl.ANY)
     vmem = pl.BlockSpec(memory_space=pltpu.VMEM)
-    smem = pl.BlockSpec(memory_space=pltpu.SMEM)
     dma = pltpu.SemaphoreType.DMA
 
     def in_hbm(x):
@@ -661,12 +665,15 @@
             pltpu.VMEM((64, 256), F32),
             pltpu.VMEM((64, 128), BF16),
         ),
-        in_specs=[any_space, any_space, any_space, vmem, smem, any_space, any_space, smem],
+        in_specs=[any_space] * 8,
         out_specs=(vmem, vmem, vmem),
         scratch_shapes=[
             pltpu.VMEM((NZ, tokens, width), BF16),
             pltpu.VMEM(base_weight.shape, BF16),
             pltpu.VMEM(delta_codes.shape, BF16),
+            pltpu.VMEM(delta_scales.shape[::-1], BF16),
+            pltpu.SMEM(owner_map.shape, jnp.int32),
+            pltpu.SMEM(lengths.shape, jnp.int32),
             pltpu.VMEM((rows * positions, kv_cache.shape[2]), BF16),
             pltpu.VMEM((tokens, queries.shape[2]), BF16),
             pltpu.VMEM((4, 64, width), BF16),
@@ -679,7 +686,7 @@
             pltpu.VMEM((NT, 80, HD), BF16),
             pltpu.VMEM((NT, 80, HD), BF16),
             pltpu.VMEM((128, 128), F32),
-            dma((5,)),
+            dma((8,)),
             dma((NZ,)),
             dma((NZ,)),
             dma((4,)),

time: 34.7 us -> 33.8 us (0.974)
  Pallas kernels: 33.9 us -> 33 us
    pallas_call x1, Pallas kernels: 32.8 us -> 31.9 us  [on_device(): pl.pallas_call(functools.partial(kernel, NG, NT), out_shape=(pltpu.VMEM((...]
where the time goes in v4:
time: 33.8 us; the launch traced here: 33.6 us
  Pallas kernels  33 us (98%)
  between operations  0.64 us (2%)
    pallas_call x1, Pallas kernels, on_device(): pl.pallas_call(functools.partial(kernel, NG, NT), out_shape=(pltpu.VMEM((...  31.9 us
    pallas_call x1, Pallas kernels, on_device(): pl.pallas_call(finish, out_shape=(jax.ShapeDtypeStruct((tokens, 128), BF1...  1.05 us

profile of v4, /device:TPU:8, one launch (start us, length us, event | category | flops | bytes accessed | tf_op | source)
XLA Modules:
  0.0 33.6 jit_solution(14442410756454615539)
XLA Ops:
  0.6 31.9 %shard_map.95 = (bf16[3,16,128]{2,1,0:T(8,128)(2,1)S(1)}, f32[64,256]{1,0:T(8,128)S(1)}, bf16[64,128]{1,0:T(8,128)(2,1)S(1)}) custom-call(bf16[16,512]{1,0:T(8,128)(2,1)} %bitcast.8, bf16[2048,512]{1,0:T(8,128)(2,1)} %base_hbm.1, bf16[64,512]{1,0:T(8,128)(2,1)} %codes_hbm.1, bf16[4,64]{1,0:T(4,128)(2,1)} %bitcast.9, s32[32]{0:T(128)} %owner_hbm.1, ...), custom_call_target="tpu_custom_call" | custom-call | tf_op jit(solution)/shard_map/pallas_call | solution.py:661
  32.6 1.1 %shard_map.96 = (bf16[16,128]{1,0:T(8,128)(2,1)}, bf16[16,512]{1,0:T(8,128)(2,1)}) custom-call(bf16[3,16,128]{2,1,0:T(8,128)(2,1)S(1)} %get-tuple-element.7.fresh_ref, f32[64,256]{1,0:T(8,128)S(1)} %get-tuple-element.8.cached_ref, bf16[64,128]{1,0:T(8,128)(2,1)S(1)} %get-tuple-element.9.own_ref), custom_call_target="tpu_custom_call" | custom-call | tf_op jit(solution)/shard_map/pallas_call | solution.py:718

commit v5 on v4

--- a/solution.py
+++ b/solution.py
@@ -43,6 +43,7 @@
     query,
     weight,
     place,
+    odd_place,
     back_send,
     back,
     base_proj,
@@ -54,6 +55,7 @@
     load_sem,
     hid_send_sem,
     hid_sem,
+    relay_send_sem,
     weight_send_sem,
     weight_sem,
     back_send_sem,
@@ -251,10 +253,37 @@
 
         return c
 
+    middle = NZ // 4
+    far = 2 * middle
+    relays = (me_z >= middle) & (me_z + middle < NZ) & (middle > 0)
+
+    def straight(z):
+        return (z != me_z + far) | (middle == 0)
+
     def start_hid_later(z, c):
-        pl.semaphore_wait(ready_z.at[z], 1)
-        hid_copy(z).start()
-        return c
+        @pl.when(straight(z))
+        def _():
+            pl.semaphore_wait(ready_z.at[z], 1)
+            hid_copy(z).start()
+
+        return c
+
+    relay_step = jnp.where(me_z < far, max(KVH // 2 - 2, middle - 1), KVH // 2 - 1)
+
+    def relay_copy():
+        z = jnp.maximum(me_z - middle, 0)
+        return pltpu.make_async_remote_copy(
+            src_ref=hid.at[z],
+            dst_ref=hid.at[z],
+            send_sem=relay_send_sem.at[0],
+            recv_sem=hid_sem.at[z],
+            device_id=(group_of(me_m, lax.rem(me_z + middle, NZ)), me_t),
+            device_id_type=MESH,
+        )
+
+    def relay():
+        wait_hid(me_z - middle)
+        relay_copy().start()
 
     start_weight(lax.rem(me_q + 2, 4))
     start_weight(3 - me_q)
@@ -265,7 +294,7 @@
     def back_copy(z):
         return pltpu.make_async_remote_copy(
             src_ref=back_send.at[z],
-            dst_ref=back.at[pl.ds(me_z * 4, 4)],
+            dst_ref=back.at[pl.ds(me_z * 2, 2)],
             send_sem=back_send_sem.at[z],
             recv_sem=back_sem.at[me_z],
             device_id=(group_of(me_m, z), me_t),
@@ -278,11 +307,15 @@
         for j in range(2):
             first = product[0:8, j * 128 : (j + 1) * 128]
             second = product[8:16, j * 128 : (j + 1) * 128]
-            back_send[z, 2 * j] = jnp.where(low, first, pltpu.roll(second, 64, 1))
-            back_send[z, 2 * j + 1] = jnp.where(low, pltpu.roll(first, 64, 1), second)
+            even = jnp.where(low, first, pltpu.roll(second, 64, 1))
+            odd = jnp.where(low, pltpu.roll(first, 64, 1), second)
+            back_send[z, j] = jnp.concatenate([even, odd], axis=0).astype(BF16)
 
     def serve(z):
-        wait_hid(z)
+        @pl.when(jnp.logical_not(relays & (z == me_z - middle)))
+        def _():
+            wait_hid(z)
+
         products(z)
         back_copy(z).start()
 
@@ -312,9 +345,10 @@
     def find(b):
         spot = jnp.int32(0)
         for g in range(NG):
-            at = ((g // 2) % NZ) * 4 + (g // (2 * NZ)) * 2 + g % 2
+            at = (((g // 2) % NZ) * 2 + g // (2 * NZ)) * 2 + g % 2
             spot = jnp.where(owner_ref[g] == b, jnp.int32(at), spot)
-        place[b] = spot
+        place[b] = lax.div(spot, jnp.int32(2))
+        odd_place[b] = lax.rem(spot, jnp.int32(2))
 
     lane = lax.broadcasted_iota(jnp.int32, (32, 128), 1)
     position = me_t * POS + lax.broadcasted_iota(jnp.int32, (64, POS), 1)
@@ -359,6 +393,10 @@
         def _():
             start_hid_later(me_z + 1 + i, 0)
 
+        @pl.when(relays & (i == relay_step) & (me_z + middle < NZ - 1))
+        def _():
+            relay()
+
         @pl.when(last & (i == 1))
         def _():
             lax.fori_loop(1, 4, wait_weight, 0)
@@ -427,6 +465,10 @@
     def _():
         start_hid_later(NZ - 1, 0)
 
+    @pl.when(relays & (me_z + middle == NZ - 1))
+    def _():
+        relay()
+
     @pl.when(jnp.logical_not(last) | (between == 0))
     def _():
         lax.fori_loop(1, 4, wait_weight, 0)
@@ -457,13 +499,13 @@
         serve(NZ - 1)
 
     products(me_z)
-    back[pl.ds(me_z * 4, 4)] = back_send[me_z]
+    back[pl.ds(me_z * 2, 2)] = back_send[me_z]
 
     def wait_back(n, c):
         z = near_peer(n)
         pltpu.make_async_remote_copy(
             src_ref=back_send.at[z],
-            dst_ref=back.at[pl.ds(z * 4, 4)],
+            dst_ref=back.at[pl.ds(z * 2, 2)],
             send_sem=back_send_sem.at[z],
             recv_sem=back_sem.at[z],
             device_id=(group_of(me_m, z), me_t),
@@ -475,9 +517,13 @@
 
     low8 = lax.broadcasted_iota(jnp.int32, (8, 128), 1) < 64
 
+    def returned(block):
+        both = back[place[block]].astype(F32)
+        return jnp.where(odd_place[block] == 0, both[0:8], both[8:16])
+
     def whole(block):
-        a = back[place[2 * block]]
-        b = back[place[2 * block + 1]]
+        a = returned(2 * block)
+        b = returned(2 * block + 1)
         first = jnp.where(low8, a, pltpu.roll(b, 64, 1))
         second = jnp.where(low8, pltpu.roll(a, 64, 1), b)
         return base_proj[block] + jnp.concatenate([first, second], axis=0)
@@ -574,8 +620,17 @@
     ).astype(BF16)
 
     def sent_z(n, c):
-        hid_copy(near_peer(n)).wait_send()
-        back_copy(near_peer(n)).wait_send()
+        z = near_peer(n)
+
+        @pl.when(straight(z))
+        def _():
+            hid_copy(z).wait_send()
+
+        @pl.when(jnp.logical_not(straight(z)))
+        def _():
+            pl.semaphore_wait(ready_z.at[z], 1)
+
+        back_copy(z).wait_send()
         return c
 
     def sent_m(i, c):
@@ -588,22 +643,31 @@
         return c
 
     lax.fori_loop(0, NZ - 1, sent_z, 0)
+
+    @pl.when(relays)
+    def _():
+        relay_copy().wait_send()
+
     lax.fori_loop(1, 4, sent_m, 0)
     lax.fori_loop(1, NT, sent_t, 0)
 
     def wait_proj(i, c):
-        u = t_peer(i)
-        pltpu.make_async_remote_copy(
-            src_ref=proj_send.at[u],
-            dst_ref=proj.at[u],
-            send_sem=proj_send_sem.at[u],
-            recv_sem=proj_sem.at[u],
-            device_id=(me_g, u),
-            device_id_type=MESH,
-        ).wait_recv()
-        return c
-
-    lax.fori_loop(1, NT, wait_proj, 0)
+        u = lax.rem(2 * (last_y + 1) + i, NT)
+
+        @pl.when(u != me_t)
+        def _():
+            pltpu.make_async_remote_copy(
+                src_ref=proj_send.at[u],
+                dst_ref=proj.at[u],
+                send_sem=proj_send_sem.at[u],
+                recv_sem=proj_sem.at[u],
+                device_id=(me_g, u),
+                device_id_type=MESH,
+            ).wait_recv()
+
+        return c
+
+    lax.fori_loop(0, NT, wait_proj, 0)
     summed = jnp.sum(proj[...].astype(F32), axis=0)
     fresh_ref[0] = (summed[0:16] + summed[16:32]).astype(BF16)
     fresh_ref[1] = summed[32:48].astype(BF16)
@@ -678,8 +742,9 @@
             pltpu.VMEM((tokens, queries.shape[2]), BF16),
             pltpu.VMEM((4, 64, width), BF16),
             pltpu.SMEM((NG,), jnp.int32),
-            pltpu.VMEM((NZ, 4, 8, 128), F32),
-            pltpu.VMEM((NZ * 4, 8, 128), F32),
+            pltpu.SMEM((NG,), jnp.int32),
+            pltpu.VMEM((NZ, 2, 16, 128), BF16),
+            pltpu.VMEM((NZ * 2, 16, 128), BF16),
             pltpu.VMEM((NT, tokens, 128), F32),
             pltpu.VMEM((NT, 4 * tokens, 128), BF16),
             pltpu.VMEM((NT, 4 * tokens, 128), BF16),
@@ -689,6 +754,7 @@
             dma((8,)),
             dma((NZ,)),
             dma((NZ,)),
+            dma((1,)),
             dma((4,)),
             dma((4,)),
             dma((NZ,)),

time: 33.8 us -> 33.3 us (0.985)
  Pallas kernels: 33 us -> 32.4 us
    pallas_call x1, Pallas kernels: 31.9 us -> 31.3 us  [on_device(): pl.pallas_call(functools.partial(kernel, NG, NT), out_shape=(pltpu.VMEM((...]
where the time goes in v5:
time: 33.3 us; the launch traced here: 33 us
  Pallas kernels  32.4 us (97%)
  between operations  0.64 us (2%)
    pallas_call x1, Pallas kernels, on_device(): pl.pallas_call(functools.partial(kernel, NG, NT), out_shape=(pltpu.VMEM((...  31.3 us
    pallas_call x1, Pallas kernels, on_device(): pl.pallas_call(finish, out_shape=(jax.ShapeDtypeStruct((tokens, 128), BF1...  1.05 us

profile of v5, /device:TPU:8, one launch (start us, length us, event | category | flops | bytes accessed | tf_op | source)
XLA Modules:
  0.0 33.0 jit_solution(14754293204295530798)
XLA Ops:
  0.6 31.3 %shard_map.95 = (bf16[3,16,128]{2,1,0:T(8,128)(2,1)S(1)}, f32[64,256]{1,0:T(8,128)S(1)}, bf16[64,128]{1,0:T(8,128)(2,1)S(1)}) custom-call(bf16[16,512]{1,0:T(8,128)(2,1)} %bitcast.8, bf16[2048,512]{1,0:T(8,128)(2,1)} %base_hbm.1, bf16[64,512]{1,0:T(8,128)(2,1)} %codes_hbm.1, bf16[4,64]{1,0:T(4,128)(2,1)} %bitcast.9, s32[32]{0:T(128)} %owner_hbm.1, ...), custom_call_target="tpu_custom_call" | custom-call | tf_op jit(solution)/shard_map/pallas_call | solution.py:725
  32.0 1.1 %shard_map.96 = (bf16[16,128]{1,0:T(8,128)(2,1)}, bf16[16,512]{1,0:T(8,128)(2,1)}) custom-call(bf16[3,16,128]{2,1,0:T(8,128)(2,1)S(1)} %get-tuple-element.7.fresh_ref, f32[64,256]{1,0:T(8,128)S(1)} %get-tuple-element.8.cached_ref, bf16[64,128]{1,0:T(8,128)(2,1)S(1)} %get-tuple-element.9.own_ref), custom_call_target="tpu_custom_call" | custom-call | tf_op jit(solution)/shard_map/pallas_call | solution.py:784

commit v6 on v5

--- a/solution.py
+++ b/solution.py
@@ -25,7 +25,7 @@
     hid_hbm,
     base_hbm,
     codes_hbm,
-    scales_hbm,
+    scales_ref,
     owner_hbm,
     cache_hbm,
     query_hbm,
@@ -36,7 +36,6 @@
     hid,
     base,
     codes,
-    scales_ref,
     owner_ref,
     lengths_ref,
     cache,
@@ -145,11 +144,9 @@
         pltpu.make_async_copy(query_hbm, query, load_sem.at[2]),
         pltpu.make_async_copy(cache_hbm, cache, load_sem.at[3]),
         pltpu.make_async_copy(base_hbm, base, load_sem.at[4]),
-        pltpu.make_async_copy(scales_hbm, scales_ref, load_sem.at[5]),
-        pltpu.make_async_copy(owner_hbm, owner_ref, load_sem.at[6]),
-        pltpu.make_async_copy(lengths_hbm, lengths_ref, load_sem.at[7]),
+        pltpu.make_async_copy(owner_hbm, owner_ref, load_sem.at[5]),
+        pltpu.make_async_copy(lengths_hbm, lengths_ref, load_sem.at[6]),
     ]
-    loads[5].start()
     loads[0].start()
     loads[1].start()
     lax.fori_loop(me_q + 1, 4, greet_m, 0)
@@ -167,7 +164,7 @@
             barrier, inc=1, device_id=(me_g, 2 * last_y + 1), device_id_type=MESH
         )
 
-    for load in loads[2:5] + loads[6:]:
+    for load in loads[2:]:
         load.start()
 
     @pl.when(greeted > 0)
@@ -184,7 +181,6 @@
     unit = (
         lax.broadcasted_iota(jnp.int32, (64, 64), 0) == lax.broadcasted_iota(jnp.int32, (64, 64), 1)
     ).astype(BF16)
-    loads[5].wait()
     scale_cols = nt_dot(unit, scales_ref[...])
     loads[0].wait()
     weight[me_m] = jnp.concatenate(
@@ -353,7 +349,7 @@
     lane = lax.broadcasted_iota(jnp.int32, (32, 128), 1)
     position = me_t * POS + lax.broadcasted_iota(jnp.int32, (64, POS), 1)
     own_rows = hid[me_z]
-    for load in loads[2:5] + loads[6:]:
+    for load in loads[2:]:
         load.wait()
 
     def cached(i, columns):
@@ -729,13 +725,12 @@
             pltpu.VMEM((64, 256), F32),
             pltpu.VMEM((64, 128), BF16),
         ),
-        in_specs=[any_space] * 8,
+        in_specs=[any_space] * 3 + [vmem] + [any_space] * 4,
         out_specs=(vmem, vmem, vmem),
         scratch_shapes=[
             pltpu.VMEM((NZ, tokens, width), BF16),
             pltpu.VMEM(base_weight.shape, BF16),
             pltpu.VMEM(delta_codes.shape, BF16),
-            pltpu.VMEM(delta_scales.shape[::-1], BF16),
             pltpu.SMEM(owner_map.shape, jnp.int32),
             pltpu.SMEM(lengths.shape, jnp.int32),
             pltpu.VMEM((rows * positions, kv_cache.shape[2]), BF16),
@@ -751,7 +746,7 @@
             pltpu.VMEM((NT, 80, HD), BF16),
             pltpu.VMEM((NT, 80, HD), BF16),
             pltpu.VMEM((128, 128), F32),
-            dma((8,)),
+            dma((7,)),
             dma((NZ,)),
             dma((NZ,)),
             dma((1,)),

time: 33.3 us -> 33.7 us (1.012)
  Pallas kernels: 32.4 us -> 32.9 us
    pallas_call x1, Pallas kernels: 31.3 us -> 31.9 us  [on_device(): pl.pallas_call(functools.partial(kernel, NG, NT), out_shape=(pltpu.VMEM((...]
where the time goes in v6:
time: 33.7 us; the launch traced here: 33.6 us
  Pallas kernels  32.9 us (98%)
  between operations  0.64 us (2%)
    pallas_call x1, Pallas kernels, on_device(): pl.pallas_call(functools.partial(kernel, NG, NT), out_shape=(pltpu.VMEM((...  31.9 us
    pallas_call x1, Pallas kernels, on_device(): pl.pallas_call(finish, out_shape=(jax.ShapeDtypeStruct((tokens, 128), BF1...  1.05 us

profile of v6, /device:TPU:8, one launch (start us, length us, event | category | flops | bytes accessed | tf_op | source)
XLA Modules:
  0.0 33.6 jit_solution(16183302556548277908)
XLA Ops:
  0.6 31.9 %shard_map.95 = (bf16[3,16,128]{2,1,0:T(8,128)(2,1)S(1)}, f32[64,256]{1,0:T(8,128)S(1)}, bf16[64,128]{1,0:T(8,128)(2,1)S(1)}) custom-call(bf16[16,512]{1,0:T(8,128)(2,1)} %bitcast.8, bf16[2048,512]{1,0:T(8,128)(2,1)} %base_hbm.1, bf16[64,512]{1,0:T(8,128)(2,1)} %codes_hbm.1, bf16[4,64]{1,0:T(4,128)(2,1)} %bitcast.9, s32[32]{0:T(128)} %owner_hbm.1, ...), custom_call_target="tpu_custom_call" | custom-call | tf_op jit(solution)/shard_map/pallas_call | solution.py:721
  32.5 1.1 %shard_map.96 = (bf16[16,128]{1,0:T(8,128)(2,1)}, bf16[16,512]{1,0:T(8,128)(2,1)}) custom-call(bf16[3,16,128]{2,1,0:T(8,128)(2,1)S(1)} %get-tuple-element.7.fresh_ref, f32[64,256]{1,0:T(8,128)S(1)} %get-tuple-element.8.cached_ref, bf16[64,128]{1,0:T(8,128)(2,1)S(1)} %get-tuple-element.9.own_ref), custom_call_target="tpu_custom_call" | custom-call | tf_op jit(solution)/shard_map/pallas_call | solution.py:779

commit v7 on v5

--- a/solution.py
+++ b/solution.py
@@ -174,8 +174,8 @@
     def _():
         pl.semaphore_wait(barrier, greeted)
 
+    lax.fori_loop(0, me_z, answer_z, 0)
     lax.fori_loop(0, me_q, answer_m, 0)
-    lax.fori_loop(0, me_z, answer_z, 0)
 
     @pl.when(at_last_y & (me_x == 1))
     def _():
@@ -268,7 +268,7 @@
 
         return c
 
-    relay_step = jnp.where(me_z < far, max(KVH // 2 - 2, middle - 1), KVH // 2 - 1)
+    relay_step = jnp.where(me_z == middle, middle - 1, jnp.where(me_z < far, max(KVH // 2 - 2, middle - 1), KVH // 2 - 1))
 
     def relay_copy():
         z = jnp.maximum(me_z - middle, 0)

time: 33.3 us -> 33.3 us (level)
  the two profiles are of different devices: /device:TPU:8 before, /device:TPU:16 now
where the time goes in v7:
time: 33.3 us; the launch traced here: 33.1 us
  Pallas kernels  32.5 us (98%)
  between operations  0.64 us (2%)
    pallas_call x1, Pallas kernels, on_device(): pl.pallas_call(functools.partial(kernel, NG, NT), out_shape=(pltpu.VMEM((...  31.4 us
    pallas_call x1, Pallas kernels, on_device(): pl.pallas_call(finish, out_shape=(jax.ShapeDtypeStruct((tokens, 128), BF1...  1.05 us

profile of v7, /device:TPU:16, one launch (start us, length us, event | category | flops | bytes accessed | tf_op | source)
XLA Modules:
  0.0 33.1 jit_solution(17088625082520447341)
XLA Ops:
  0.6 31.4 %shard_map.95 = (bf16[3,16,128]{2,1,0:T(8,128)(2,1)S(1)}, f32[64,256]{1,0:T(8,128)S(1)}, bf16[64,128]{1,0:T(8,128)(2,1)S(1)}) custom-call(bf16[16,512]{1,0:T(8,128)(2,1)} %bitcast.8, bf16[2048,512]{1,0:T(8,128)(2,1)} %base_hbm.1, bf16[64,512]{1,0:T(8,128)(2,1)} %codes_hbm.1, bf16[4,64]{1,0:T(4,128)(2,1)} %bitcast.9, s32[32]{0:T(128)} %owner_hbm.1, ...), custom_call_target="tpu_custom_call" | custom-call | tf_op jit(solution)/shard_map/pallas_call | solution.py:725
  32.1 1.1 %shard_map.96 = (bf16[16,128]{1,0:T(8,128)(2,1)}, bf16[16,512]{1,0:T(8,128)(2,1)}) custom-call(bf16[3,16,128]{2,1,0:T(8,128)(2,1)S(1)} %get-tuple-element.7.fresh_ref, f32[64,256]{1,0:T(8,128)S(1)} %get-tuple-element.8.cached_ref, bf16[64,128]{1,0:T(8,128)(2,1)S(1)} %get-tuple-element.9.own_ref), custom_call_target="tpu_custom_call" | custom-call | tf_op jit(solution)/shard_map/pallas_call | solution.py:784

commit v8 on v5

--- a/solution.py
+++ b/solution.py
@@ -356,6 +356,10 @@
     for load in loads[2:5] + loads[6:]:
         load.wait()
 
+    def tell(i, c):
+        pl.semaphore_signal(ready_t, inc=1, device_id=(me_g, t_peer(i)), device_id_type=MESH)
+        return c
+
     def cached(i, columns):
         for n in range(2):
             k = 2 * i + n
@@ -393,6 +397,11 @@
         def _():
             start_hid_later(me_z + 1 + i, 0)
 
+        @pl.when(herald & (i == 0))
+        def _():
+            pl.semaphore_wait(ready_x, 1)
+            lax.fori_loop(1, NT, tell, 0)
+
         @pl.when(relays & (i == relay_step) & (me_z + middle < NZ - 1))
         def _():
             relay()
@@ -406,15 +415,6 @@
             serve(i - 1)
 
         return columns
-
-    def tell(i, c):
-        pl.semaphore_signal(ready_t, inc=1, device_id=(me_g, t_peer(i)), device_id_type=MESH)
-        return c
-
-    @pl.when(herald)
-    def _():
-        pl.semaphore_wait(ready_x, 1)
-        lax.fori_loop(1, NT, tell, 0)
 
     lse_cols[...] = jnp.zeros_like(lse_cols)
     lse_cols[0:32] = lax.fori_loop(0, KVH // 2, cached, jnp.zeros((32, 128), F32))

time: 33.3 us -> 33.3 us (level)
  the two profiles are of different devices: /device:TPU:8 before, /device:TPU:2 now
where the time goes in v8:
time: 33.3 us; the launch traced here: 33.2 us
  Pallas kernels  32.6 us (98%)
  between operations  0.64 us (2%)
    pallas_call x1, Pallas kernels, on_device(): pl.pallas_call(functools.partial(kernel, NG, NT), out_shape=(pltpu.VMEM((...  31.5 us
    pallas_call x1, Pallas kernels, on_device(): pl.pallas_call(finish, out_shape=(jax.ShapeDtypeStruct((tokens, 128), BF1...  1.05 us

profile of v8, /device:TPU:2, one launch (start us, length us, event | category | flops | bytes accessed | tf_op | source)
XLA Modules:
  0.0 33.2 jit_solution(8820553754502273614)
XLA Ops:
  0.6 31.5 %shard_map.95 = (bf16[3,16,128]{2,1,0:T(8,128)(2,1)S(1)}, f32[64,256]{1,0:T(8,128)S(1)}, bf16[64,128]{1,0:T(8,128)(2,1)S(1)}) custom-call(bf16[16,512]{1,0:T(8,128)(2,1)} %bitcast.8, bf16[2048,512]{1,0:T(8,128)(2,1)} %base_hbm.1, bf16[64,512]{1,0:T(8,128)(2,1)} %codes_hbm.1, bf16[4,64]{1,0:T(4,128)(2,1)} %bitcast.9, s32[32]{0:T(128)} %owner_hbm.1, ...), custom_call_target="tpu_custom_call" | custom-call | tf_op jit(solution)/shard_map/pallas_call | solution.py:725
  32.1 1.1 %shard_map.96 = (bf16[16,128]{1,0:T(8,128)(2,1)}, bf16[16,512]{1,0:T(8,128)(2,1)}) custom-call(bf16[3,16,128]{2,1,0:T(8,128)(2,1)S(1)} %get-tuple-element.7.fresh_ref, f32[64,256]{1,0:T(8,128)S(1)} %get-tuple-element.8.cached_ref, bf16[64,128]{1,0:T(8,128)(2,1)S(1)} %get-tuple-element.9.own_ref), custom_call_target="tpu_custom_call" | custom-call | tf_op jit(solution)/shard_map/pallas_call | solution.py:784
